TPU v7x, 512 devices: a whole 4x8x8 slice. The times are simulated.
512 devices in a mesh: grp: 8 (over z), dom: 64 (over x, y, core).
Axes of the slice: x: 4, y: 8, z: 8, core: 2. Of those that a mesh axis runs over, the one named last changes fastest.
Arguments:
- features: bfloat16 [65536, 512], P(('grp', 'dom')), may hold values from -6 to 6
- w_self: bfloat16 [512, 512], replicated, may hold values from -0.25 to 0.25
- w_neigh: bfloat16 [512, 512], replicated, may hold values from -1 to 1
- cotangent: bfloat16 [65536, 512], P(('grp', 'dom')), may hold values from -6 to 6
- neighbors: int32 [65536, 16], P(('grp', 'dom')), may hold values from 0 to 639, as said below
- send_rows: int32 [8, 64, 64, 8], P('grp', 'dom'), may hold values from 0 to 127, as said below
- send_count: int32 [8, 64, 64], P('grp', 'dom'), may hold values from 1 to 8, as said below
Outputs:
- grad_features: bfloat16 [65536, 512], P(('grp', 'dom'))
- grad_w_self: float32 [512, 512], replicated
- grad_w_neigh: float32 [512, 512], replicated
Inputs may be any that keep to these rules, and one draw needn't show every extreme that they name: `send_rows`: within one (g, p, d) the 8 slots name distinct rows. `send_count`: every partition receives the full 8 from at least one sender of its group. `neighbors`: in each row the first 8 entries name own rows of the node's partition; the others are 128 + p * 8 + s, a live slot s of peer p's boundary rows to that partition.
All inputs are finite; a program needn't handle non-finite values.
Results may differ from a plain program's by a relative error of at most 0.0063.
Values may be sent and summed in bfloat16 or wider, within the bound.
A program may use at most 64 MiB of HBM per device.

v0:
```python
import jax
import jax.numpy as jnp
from jax import lax
from jax.sharding import PartitionSpec as P


def contract_first(left, right):
    return lax.dot_general(
        left, right, (((0,), (0,)), ((), ())), preferred_element_type=jnp.float32
    )


def contract_last(left, right):
    return lax.dot_general(
        left, right, (((1,), (1,)), ((), ())), preferred_element_type=jnp.float32
    )


def count_matrix(entries, columns):
    column_ids = lax.broadcasted_iota(jnp.int32, (1, 1, columns), 2)
    return jnp.sum(entries[:, :, None] == column_ids, axis=1).astype(jnp.bfloat16)


def local(features, w_self, w_neigh, cotangent, neighbors, send_rows, send_count):
    node_count = features.shape[0]
    feature_width = features.shape[1]
    peer_count = lax.axis_size("dom")
    slot_count = send_rows.shape[3]
    degree = neighbors.shape[1]
    half_degree = degree // 2
    halo_width = peer_count * slot_count
    row_ids = send_rows.reshape(halo_width)
    live_counts = send_count.reshape(peer_count)
    live_slots = (
        lax.broadcasted_iota(jnp.int32, (peer_count, slot_count), 1) < live_counts[:, None]
    ).reshape(halo_width)
    node_ids = lax.broadcasted_iota(jnp.int32, (1, node_count), 1)
    selector = ((row_ids[:, None] == node_ids) & live_slots[:, None]).astype(jnp.bfloat16)
    outgoing = jnp.dot(selector, features, preferred_element_type=jnp.float32).astype(jnp.bfloat16)
    outgoing = outgoing.reshape(peer_count, slot_count, feature_width)
    incoming = lax.all_to_all(outgoing, "dom", split_axis=0, concat_axis=0, tiled=True).reshape(
        halo_width, feature_width
    )
    own_adjacency = count_matrix(neighbors[:, :half_degree], node_count)
    halo_adjacency = count_matrix(neighbors[:, half_degree:] - node_count, halo_width)
    summed = jnp.dot(own_adjacency, features, preferred_element_type=jnp.float32) + jnp.dot(
        halo_adjacency, incoming, preferred_element_type=jnp.float32
    )
    aggregate = (summed / degree).astype(jnp.bfloat16)
    pre_act = jnp.dot(features, w_self, preferred_element_type=jnp.float32) + jnp.dot(
        aggregate, w_neigh, preferred_element_type=jnp.float32
    )
    _, backward = jax.vjp(jax.nn.gelu, pre_act)
    grad_pre = backward(cotangent.astype(jnp.float32))[0].astype(jnp.bfloat16)
    grad_scale = float(node_count * lax.axis_size("grp") * peer_count) ** (-0.5)
    stacked = (
        jnp.stack([contract_first(features, grad_pre), contract_first(aggregate, grad_pre)])
        * grad_scale
    )
    summed_grads = lax.psum(stacked, ("grp", "dom"))
    grad_agg = (contract_last(grad_pre, w_neigh) / degree).astype(jnp.bfloat16)
    grad_rows = contract_last(grad_pre, w_self) + contract_first(own_adjacency, grad_agg)
    halo_grad = contract_first(halo_adjacency, grad_agg).astype(jnp.bfloat16)
    halo_grad = halo_grad.reshape(peer_count, slot_count, feature_width)
    returned = lax.all_to_all(halo_grad, "dom", split_axis=0, concat_axis=0, tiled=True).reshape(
        halo_width, feature_width
    )
    grad_rows = grad_rows + contract_first(selector, returned)
    return (grad_rows.astype(jnp.bfloat16), summed_grads[0], summed_grads[1])


def solution(mesh):
    placed = (
        P(("grp", "dom"), None),
        P(),
        P(),
        P(("grp", "dom"), None),
        P(("grp", "dom"), None),
        P("grp", "dom", None, None),
        P("grp", "dom", None),
    )
    return jax.shard_map(
        local,
        mesh=mesh,
        in_specs=placed,
        out_specs=(P(("grp", "dom"), None), P(), P()),
        check_vma=False,
    )
```

profile of v0, /device:TPU:1, one launch (start us, length us, event | category | flops | bytes accessed | tf_op | source)
XLA Modules:
  0.0 349.5 jit_solution(9976546286541100842)
XLA Ops:
  7.2 0.8 iota_compare_fusion.3
  8.1 0.8 copy.23
  9.0 2.1 fusion
  11.0 11.8 %all-to-all-start = ((bf16[64,8,512]{2,1,0:T(8,128)(2,1)}), bf16[64,8,512]{2,1,0:T(8,128)(2,1)S(1)}, u32[]{:S(2)}, u32[]{:S(2)}) async-start(bf16[64,8,512]{2,1,0:T(8,128)(2,1)} %fusion), calls=%async_computation | async-start | bytes 1048576 | tf_op jit(solution)/shard_map/all_to_all | solution.py:41
  22.8 0.7 slice_add_fusion
  23.7 0.2 convert_reduce_fusion.1
  24.0 0.7 convert_reduce_fusion
  24.8 0.2 fusion.30
  25.1 15.1 %all-to-all-done = bf16[64,8,512]{2,1,0:T(8,128)(2,1)S(1)} async-done(((bf16[64,8,512]{2,1,0:T(8,128)(2,1)}), bf16[64,8,512]{2,1,0:T(8,128)(2,1)S(1)}, u32[]{:S(2)}, u32[]{:S(2)}) %all-to-all-start) | async-done | bytes 524320 | tf_op jit(solution)/shard_map/all_to_all | solution.py:41
  40.1 0.2 fusion.5
  40.4 0.4 fusion.10
  40.8 0.3 fusion.3
  41.1 0.3 convolution_bitcast_fusion
  41.5 1.1 fusion.1
  42.6 6.3 %all-to-all-start.1 = ((bf16[64,8,512]{2,1,0:T(8,128)(2,1)}), bf16[64,8,512]{2,1,0:T(8,128)(2,1)S(1)}, u32[]{:S(2)}, u32[]{:S(2)}) async-start(bf16[64,8,512]{2,1,0:T(8,128)(2,1)} %fusion.1), calls=%async_computation.1 | async-start | bytes 1048576 | tf_op jit(solution)/shard_map/all_to_all | solution.py:65
  48.9 0.3 convolution_bitcast_fusion.1
  49.2 1.5 maximum_multiply_fusion
  50.8 0.3 fusion.31
  51.3 14.9 %all-to-all-done.1 = bf16[64,8,512]{2,1,0:T(8,128)(2,1)S(1)} async-done(((bf16[64,8,512]{2,1,0:T(8,128)(2,1)}), bf16[64,8,512]{2,1,0:T(8,128)(2,1)S(1)}, u32[]{:S(2)}, u32[]{:S(2)}) %all-to-all-start.1) | async-done | bytes 524320 | tf_op jit(solution)/shard_map/all_to_all | solution.py:65
  66.2 1.1 fusion.4
  67.3 271.1 %all-reduce.2.cloned.1.call-done = f32[2,512,512]{1,2,0:T(8,128)} async-done(((f32[2,512,512]{1,2,0:T(8,128)}), f32[2,512,512]{1,2,0:T(8,128)}) %all-reduce.2.cloned.1.call-update) | async-done | bytes 2097168 | tf_op jit(solution)/shard_map/psum | solution.py:60
  338.4 1.7 slice_bitcast_fusion
  340.1 1.3 copy.26
  341.4 1.3 copy.25
  (16 shorter events, 0.8 us)
Async XLA Ops:
  7.2 33.2 %copy-start = (bf16[512,512]{1,0:T(8,128)(2,1)S(1)}, bf16[512,512]{1,0:T(8,128)(2,1)}, u32[]{:S(2)}) copy-start(bf16[512,512]{1,0:T(8,128)(2,1)} %param.9) | copy-start | bytes 1572868
  7.2 17.5 %copy-start.2 = (bf16[128,512]{1,0:T(8,128)(2,1)S(1)}, bf16[128,512]{1,0:T(8,128)(2,1)}, u32[]{:S(2)}) copy-start(bf16[128,512]{1,0:T(8,128)(2,1)} %param.7) | copy-start | bytes 393220
  7.2 17.6 %copy-start.1 = (bf16[512,512]{1,0:T(8,128)(2,1)S(1)}, bf16[512,512]{1,0:T(8,128)(2,1)}, u32[]{:S(2)}) copy-start(bf16[512,512]{1,0:T(8,128)(2,1)} %param.8) | copy-start | bytes 1572868
  11.0 29.3 %copy-start.3 = (bf16[128,512]{1,0:T(8,128)(2,1)S(1)}, bf16[128,512]{1,0:T(8,128)(2,1)}, u32[]{:S(2)}) copy-start(bf16[128,512]{1,0:T(8,128)(2,1)} %param.10) | copy-start | bytes 393220
  11.0 29.1 %all-to-all-start = ((bf16[64,8,512]{2,1,0:T(8,128)(2,1)}), bf16[64,8,512]{2,1,0:T(8,128)(2,1)S(1)}, u32[]{:S(2)}, u32[]{:S(2)}) async-start(bf16[64,8,512]{2,1,0:T(8,128)(2,1)} %fusion), calls=%async_computation | async-start | bytes 1048576 | tf_op jit(solution)/shard_map/all_to_all | solution.py:41
  42.6 23.6 %all-to-all-start.1 = ((bf16[64,8,512]{2,1,0:T(8,128)(2,1)}), bf16[64,8,512]{2,1,0:T(8,128)(2,1)S(1)}, u32[]{:S(2)}, u32[]{:S(2)}) async-start(bf16[64,8,512]{2,1,0:T(8,128)(2,1)} %fusion.1), calls=%async_computation.1 | async-start | bytes 1048576 | tf_op jit(solution)/shard_map/all_to_all | solution.py:65
  48.9 289.5 %all-reduce.2.cloned.1.call-start = ((), (), s32[]{:S(2)}) async-start(), calls=%async_computation.2 | async-start | bytes 4194304 | tf_op jit(solution)/shard_map/psum | solution.py:60
Sparse Core Ops, SparseCore 0:
  54.6 283.6 all-reduce.1
where the time goes:
time: 350 us
  waiting for transfers between devices  301 us (86%)
  starting transfers between devices  18.1 us (5%)
  between operations  14.2 us (4%)
  matrix products  6.74 us (2%)
  local copies, waits for them, and re-layouts  5.51 us (2%)
  other arithmetic  3.98 us (1%)
    psum x1, waiting for transfers between devices, local(): summed_grads = lax.psum(stacked, ('grp', 'dom'))  271 us
    all_to_all x1, waiting for transfers between devices, local(): lax.all_to_all(outgoing, 'dom', split_axis=0, concat_axis=0, tiled=True)  15.1 us
    all_to_all x1, waiting for transfers between devices, local(): lax.all_to_all(halo_grad, 'dom', split_axis=0, concat_axis=0, tiled=True)  14.9 us
    all_to_all x1, starting transfers between devices, local(): lax.all_to_all(outgoing, 'dom', split_axis=0, concat_axis=0, tiled=True)  11.8 us
  transfers between devices with their start and end apart: 3, of which 3 were waited for; matrix products, arithmetic and copies ran while one was open for 2% of the time, Pallas kernels for 0%

commit v1 on v0

v1 whole, which is shorter than its diff:
```python
import functools

import jax
import jax.numpy as jnp
from jax import lax
from jax.experimental import pallas as pl
from jax.experimental.pallas import tpu as pltpu
from jax.sharding import PartitionSpec as P

MESH = pl.DeviceIdType.MESH
F32 = jnp.float32
BF16 = jnp.bfloat16


def dot(left, right, left_dim=1, right_dim=0):
    return lax.dot_general(
        left, right, (((left_dim,), (right_dim,)), ((), ())), preferred_element_type=F32
    )


def iota(shape, dim):
    return lax.broadcasted_iota(jnp.int32, shape, dim)


def gelu_slope(v):
    root = 0.7978845608028654
    square = v * v
    t = jnp.tanh(root * (v + 0.044715 * square * v))
    return 0.5 * (1.0 + t) + (0.5 * root) * v * (1.0 - t * t) * (1.0 + 0.134145 * square)


def kernel(
    feat_ref, ws_ref, wn_ref, cot_ref, nb_ref, rows_ref, count_ref,
    gfeat_ref, gw_ref,
    sel_ref, adj_ref, adjt_ref, out_ref, halo_ref, back_ref, ret_ref,
    lt_ref, own_ref, pair_out, pair_in, z_out, z_in, xy_out, xy_in, ag_ref, agz_ref, full_ref, base_ref,
    a2a_send, a2a_recv, pair_send, pair_recv, z_send, z_recv, xy_send, xy_recv,
    ag1_send, ag1_recv, ag2_send, ag2_recv, fin_send, fin_recv,
):
    grp = lax.axis_index("grp")
    dom = lax.axis_index("dom")
    core = lax.rem(dom, 2)
    place = dom // 2
    other = 1 - core
    sibling = dom + 1 - 2 * core

    def dom_peer(r):
        return lax.rem(dom + r, 64)

    def grp_peer(r):
        return lax.rem(grp + r, 8)

    def place_peer(r):
        return lax.rem(place + r, 32)

    def loop(first, last, body):
        lax.fori_loop(first, last, lambda i, c: (body(i), c)[1], 0)

    def remote(src, dst, send, recv, device):
        return pltpu.make_async_remote_copy(
            src_ref=src, dst_ref=dst, send_sem=send, recv_sem=recv,
            device_id=device, device_id_type=MESH,
        )

    def wait(ref, sem):
        pltpu.make_async_copy(ref, ref, sem).wait()

    barrier = pltpu.get_barrier_semaphore()
    loop(1, 64, lambda r: pl.semaphore_signal(
        barrier, inc=1, device_id={"dom": dom_peer(r)}, device_id_type=MESH))
    loop(1, 8, lambda r: pl.semaphore_signal(
        barrier, inc=1, device_id={"grp": grp_peer(r)}, device_id_type=MESH))

    col = iota((1, 1024), 1)
    slot_of = jnp.bitwise_and(col, 7)
    half_of = jnp.bitwise_and(lax.shift_right_logical(col, 3), 1)
    peer_of = lax.shift_right_logical(col, 4)
    in_peer = iota((64, 1024), 0) == peer_of
    in_slot = (iota((8, 1024), 0) == slot_of).astype(BF16)
    spread = dot(rows_ref[...].astype(F32).astype(BF16), in_slot)
    row = jnp.sum(jnp.where(in_peer, spread, 0.0), axis=0, keepdims=True)
    counts = jnp.broadcast_to(count_ref[...], (8, 64)).astype(F32).astype(BF16)
    live = dot(counts, in_peer.astype(BF16))[0:1] > slot_of.astype(F32)
    target = jnp.where(live, row + 128.0 * half_of.astype(F32), 512.0)
    sel_ref[...] = (iota((256, 1024), 0).astype(F32) == target).astype(BF16)
    feat = feat_ref[...]
    feat2 = jnp.concatenate([feat[:, :256], feat[:, 256:]], axis=0)
    out_ref[...] = dot(sel_ref[...], feat2, 0, 0).astype(BF16)

    pl.semaphore_wait(barrier, 70)

    def block(ref, i):
        return ref.at[pl.ds(pl.multiple_of(i * 16, 16), 16)]

    def send_boundary(src, dst, k):
        def one(r):
            peer = dom_peer(r)
            remote(block(src, peer), block(dst, dom), a2a_send.at[k], a2a_recv.at[k],
                   {"dom": peer}).start()
        loop(1, 64, one)

    def wait_boundary(src, dst, k):
        wait(dst.at[pl.ds(0, 63 * 16)], a2a_recv.at[k])

    send_boundary(out_ref, halo_ref, 0)
    halo_ref[pl.ds(pl.multiple_of(dom * 16, 16), 16), :] = out_ref[
        pl.ds(pl.multiple_of(dom * 16, 16), 16), :]

    nb = nb_ref[...]
    entry = nb - 128
    place_of = lax.shift_left(lax.shift_right_arithmetic(entry, 3), 4) + jnp.bitwise_and(entry, 7)
    column_ids = iota((128, 1024), 1)
    count = jnp.zeros((128, 1024), F32)
    for k in range(8, 16):
        count = count + jnp.where(column_ids == place_of[:, k:k + 1], 1.0, 0.0)
    upper = pltpu.roll(count, 8, 1)
    adj_ref[0:128, :] = count.astype(BF16)
    adj_ref[128:256, :] = upper.astype(BF16)
    adjt_ref[:, 0:128] = count.T.astype(BF16)
    adjt_ref[:, 128:256] = upper.T.astype(BF16)
    own_ids = iota((128, 128), 1)
    own = jnp.zeros((128, 128), F32)
    for k in range(8):
        own = own + jnp.where(own_ids == nb[:, k:k + 1], 1.0, 0.0)
    own_adj = own.astype(BF16)
    own_adj_t = own.T.astype(BF16)
    own_sum = dot(own_adj, feat)
    pre_self = dot(feat, ws_ref[...])
    lt_ref[0] = feat.astype(F32).T.astype(BF16)

    wait_boundary(out_ref, halo_ref, 0)
    halo_sum = dot(adj_ref[...], halo_ref[...])
    summed = own_sum + jnp.concatenate([halo_sum[0:128], halo_sum[128:256]], axis=1)
    agg = (summed * (1.0 / 16.0)).astype(BF16)
    pre = pre_self + dot(agg, wn_ref[...])
    grad_pre = (cot_ref[...].astype(F32) * gelu_slope(pre)).astype(BF16)

    agg_t = agg.astype(F32).T
    agg_t = jnp.swapaxes(agg_t.reshape(8, 8, 8, 128), 0, 1).reshape(512, 128)
    lt_ref[1] = agg_t.astype(BF16)
    scale = 65536.0 ** -0.5
    pair_out[...] = (dot(lt_ref[other], grad_pre) * scale).astype(BF16)

    def chunk(ref, i):
        return ref.at[pl.ds(pl.multiple_of(i * 64, 64), 64)]

    def send_pair(r):
        i = grp_peer(r)
        remote(chunk(pair_out, i), chunk(pair_in, i), pair_send.at[i], pair_recv.at[i],
               {"dom": sibling}).start()
    loop(1, 9, send_pair)
    own_ref[...] = dot(lt_ref[core], grad_pre) * scale

    grad_agg = (dot(grad_pre, wn_ref[...], 1, 1) * (1.0 / 16.0)).astype(BF16)
    grad_agg2 = jnp.concatenate([grad_agg[:, :256], grad_agg[:, 256:]], axis=0)
    back_ref[...] = dot(adjt_ref[...], grad_agg2).astype(BF16)

    def send_z(r):
        i = grp_peer(r)
        wait(chunk(pair_in, i), pair_recv.at[i])
        at = pl.ds(pl.multiple_of(i * 64, 64), 64)
        z_out[at, :] = (own_ref[at, :] + pair_in[at, :].astype(F32)).astype(BF16)
        remote(chunk(z_out, i), chunk(z_in, grp), z_send, z_recv, {"grp": i}).start()
    loop(1, 8, send_z)

    send_boundary(back_ref, ret_ref, 1)
    ret_ref[pl.ds(pl.multiple_of(dom * 16, 16), 16), :] = back_ref[
        pl.ds(pl.multiple_of(dom * 16, 16), 16), :]
    base_ref[...] = dot(grad_pre, ws_ref[...], 1, 1) + dot(own_adj_t, grad_agg)

    wait(chunk(pair_in, grp), pair_recv.at[grp])
    mine = pl.ds(pl.multiple_of(grp * 64, 64), 64)
    total = own_ref[mine, :] + pair_in[mine, :].astype(F32)
    wait(z_in.at[pl.ds(0, 7 * 64)], z_recv)
    for r in range(1, 8):
        total = total + z_in[pl.ds(pl.multiple_of(grp_peer(r) * 64, 64), 64), :].astype(F32)

    for q in range(32):
        a, b = q // 4, q % 4
        xy_out[q] = total[8 * a:8 * a + 8, 128 * b:128 * b + 128]

    def send_xy(r):
        q = place_peer(r)
        remote(xy_out.at[q], xy_in.at[place], xy_send, xy_recv, {"dom": 2 * q + core}).start()
    loop(1, 32, send_xy)

    wait_boundary(back_ref, ret_ref, 1)
    returned = dot(sel_ref[...], ret_ref[...])
    gfeat_ref[...] = (
        base_ref[...] + jnp.concatenate([returned[0:128], returned[128:256]], axis=1)
    ).astype(BF16)

    wait(xy_in.at[pl.ds(0, 31)], xy_recv)
    xy_in[place] = xy_out[place]
    done = jnp.sum(xy_in[...], axis=0)

    @pl.when(core == 0)
    def _():
        ag_ref[place] = done

        def send_one(r):
            q = place_peer(r)
            remote(ag_ref.at[place], ag_ref.at[place], ag1_send, ag1_recv, {"dom": 2 * q}).start()
        loop(1, 32, send_one)
        wait(ag_ref.at[pl.ds(0, 31)], ag1_recv)
        wait(ag_ref.at[pl.ds(0, 31)], ag1_send)
        rows = [jnp.concatenate([ag_ref[4 * a + b] for b in range(4)], axis=1) for a in range(8)]
        full_ref[0, mine, :] = jnp.concatenate(rows, axis=0).astype(BF16)

        def send_two(r):
            remote(full_ref.at[0, mine], full_ref.at[0, mine], ag2_send, ag2_recv,
                   {"grp": grp_peer(r)}).start()
        loop(1, 8, send_two)
        wait(full_ref.at[0, pl.ds(0, 7 * 64)], ag2_recv)
        wait(full_ref.at[0, pl.ds(0, 7 * 64)], ag2_send)

    @pl.when(core == 1)
    def _():
        agz_ref[grp] = done

        def send_one(r):
            remote(agz_ref.at[grp], agz_ref.at[grp], ag1_send, ag1_recv,
                   {"grp": grp_peer(r)}).start()
        loop(1, 8, send_one)
        wait(agz_ref.at[pl.ds(0, 7)], ag1_recv)
        wait(agz_ref.at[pl.ds(0, 7)], ag1_send)
        a = place // 4
        b = lax.rem(place, 4)
        at = (pl.ds(pl.multiple_of(a * 64, 64), 64), pl.ds(pl.multiple_of(b * 128, 128), 128))
        full_ref[1, at[0], at[1]] = agz_ref[...].reshape(64, 128).astype(BF16)

        def send_two(r):
            q = place_peer(r)
            remote(full_ref.at[1, at[0], at[1]], full_ref.at[1, at[0], at[1]], ag2_send, ag2_recv,
                   {"dom": 2 * q + 1}).start()
        loop(1, 32, send_two)
        wait(full_ref.at[1, pl.ds(0, 496)], ag2_recv)
        wait(full_ref.at[1, pl.ds(0, 496)], ag2_send)

    last = remote(full_ref.at[core], full_ref.at[core], fin_send, fin_recv, {"dom": sibling})
    last.start()

    wait(out_ref.at[pl.ds(0, 63 * 16)], a2a_send.at[0])
    wait(back_ref.at[pl.ds(0, 63 * 16)], a2a_send.at[1])
    loop(0, 8, lambda i: wait(chunk(pair_out, i), pair_send.at[i]))
    wait(z_out.at[pl.ds(0, 7 * 64)], z_send)
    wait(xy_out.at[pl.ds(0, 31)], xy_send)
    last.wait()
    gw_ref[...] = full_ref[...]


def local(features, w_self, w_neigh, cotangent, neighbors, send_rows, send_count):
    vmem = pl.BlockSpec(memory_space=pltpu.VMEM)
    dma = pltpu.SemaphoreType.DMA
    grad_features, grads = pl.pallas_call(
        kernel,
        out_shape=(
            jax.ShapeDtypeStruct((128, 512), BF16),
            jax.ShapeDtypeStruct((2, 512, 512), BF16),
        ),
        in_specs=[vmem] * 7,
        out_specs=(vmem, vmem),
        scratch_shapes=[
            pltpu.VMEM((256, 1024), BF16),
            pltpu.VMEM((256, 1024), BF16),
            pltpu.VMEM((1024, 256), BF16),
            pltpu.VMEM((1024, 256), BF16),
            pltpu.VMEM((1024, 256), BF16),
            pltpu.VMEM((1024, 256), BF16),
            pltpu.VMEM((1024, 256), BF16),
            pltpu.VMEM((2, 512, 128), BF16),
            pltpu.VMEM((512, 512), F32),
            pltpu.VMEM((512, 512), BF16),
            pltpu.VMEM((512, 512), BF16),
            pltpu.VMEM((512, 512), BF16),
            pltpu.VMEM((512, 512), BF16),
            pltpu.VMEM((32, 8, 128), F32),
            pltpu.VMEM((32, 8, 128), F32),
            pltpu.VMEM((32, 8, 128), F32),
            pltpu.VMEM((8, 8, 128), F32),
            pltpu.VMEM((2, 512, 512), BF16),
            pltpu.VMEM((128, 512), F32),
            dma((2,)), dma((2,)), dma((8,)), dma((8,)), dma, dma, dma, dma,
            dma, dma, dma, dma, dma, dma,
        ],
        compiler_params=pltpu.CompilerParams(
            collective_id=0, has_side_effects=True, vmem_limit_bytes=40 << 20
        ),
        name="sage_backward",
    )(
        features, w_self, w_neigh, cotangent, neighbors,
        send_rows.reshape(64, 8), send_count.reshape(1, 64),
    )
    return grad_features, grads[0].astype(F32), grads[1].astype(F32)


def solution(mesh):
    placed = (
        P(("grp", "dom"), None),
        P(),
        P(),
        P(("grp", "dom"), None),
        P(("grp", "dom"), None),
        P("grp", "dom", None, None),
        P("grp", "dom", None),
    )
    return jax.shard_map(
        local,
        mesh=mesh,
        in_specs=placed,
        out_specs=(P(("grp", "dom"), None), P(), P()),
        check_vma=False,
    )
```

time: 350 us -> 80.4 us (0.23)
  waiting for transfers between devices: 301 us -> 0 us
  Pallas kernels: 0 us -> 71.9 us
  starting transfers between devices: 18.1 us -> 0 us
  between operations: 14.2 us -> 0.66 us
  matrix products: 6.74 us -> 0 us
    psum x1 -> x0, waiting for transfers between devices: 271 us -> none  [local(): summed_grads = lax.psum(stacked, ('grp', 'dom'))]
    pallas_call x0 -> x1, Pallas kernels: none -> 71.9 us  [local(): pl.pallas_call(kernel, out_shape=(jax.ShapeDtypeStruct((128, 512), BF16),...]
    all_to_all x2 -> x0, waiting for transfers between devices: 29.9 us -> none  [the longest x1 15.1 us: local(): lax.all_to_all(outgoing, 'dom', split_axis=0, concat_axis=0, tiled=True)]
    all_to_all x2 -> x0, starting transfers between devices: 18 us -> none  [the longest x1 11.8 us: local(): lax.all_to_all(outgoing, 'dom', split_axis=0, concat_axis=0, tiled=True)]
    dot_general x12 -> x0, matrix products: 6.74 us -> none  [the longest x5 3.07 us: contract_first(): lax.dot_general(left, right, (((0,), (0,)), ((), ())), preferred_element_...]
  transfers between devices with their start and end apart: 3 -> 0, of which waited for: 3 -> 0; matrix products, arithmetic and copies ran while one was open for 2% -> 0% of each run, Pallas kernels for 0% -> 0%
where the time goes in v1:
time: 80.4 us; the launch traced here: 80.1 us
  Pallas kernels  71.9 us (89%)
  local copies, waits for them, and re-layouts  5.97 us (7%)
  other arithmetic  1.6 us (2%)
    pallas_call x1, Pallas kernels, local(): pl.pallas_call(kernel, out_shape=(jax.ShapeDtypeStruct((128, 512), BF16),...  71.9 us
    unnamed x15, local copies, waits for them, and re-layouts  5.97 us

profile of v1, /device:TPU:1, one launch (start us, length us, event | category | flops | bytes accessed | tf_op | source)
XLA Modules:
  0.0 80.1 jit_solution(9458483105111732363)
XLA Ops:
  0.6 0.0 copy-start.5
  0.6 0.8 copy.10
  1.4 0.0 copy-done.5
  1.4 0.0 copy-start.4
  1.4 0.1 copy.11.nb_ref
  1.5 0.5 copy-done.4
  2.1 0.0 copy-start
  2.1 1.0 %copy-done = bf16[512,512]{1,0:T(8,128)(2,1)S(1)} copy-done((bf16[512,512]{1,0:T(8,128)(2,1)S(1)}, bf16[512,512]{1,0:T(8,128)(2,1)}, u32[]{:S(2)}) %copy-start) | copy-done | bytes 524312
  3.1 0.0 copy-start.1
  3.1 1.0 %copy-done.1 = bf16[512,512]{1,0:T(8,128)(2,1)S(1)} copy-done((bf16[512,512]{1,0:T(8,128)(2,1)S(1)}, bf16[512,512]{1,0:T(8,128)(2,1)}, u32[]{:S(2)}) %copy-start.1) | copy-done | bytes 524312
  4.2 0.0 copy-start.2
  4.2 0.9 %copy-done.2 = bf16[128,512]{1,0:T(8,128)(2,1)S(1)} copy-done((bf16[128,512]{1,0:T(8,128)(2,1)S(1)}, bf16[128,512]{1,0:T(8,128)(2,1)}, u32[]{:S(2)}) %copy-start.2) | copy-done | bytes 131096
  5.1 0.0 copy-start.3
  5.1 0.9 %copy-done.3 = bf16[128,512]{1,0:T(8,128)(2,1)S(1)} copy-done((bf16[128,512]{1,0:T(8,128)(2,1)S(1)}, bf16[128,512]{1,0:T(8,128)(2,1)}, u32[]{:S(2)}) %copy-start.3) | copy-done | bytes 131096
  6.0 71.9 %sage_backward.1 = (bf16[128,512]{1,0:T(8,128)(2,1)S(1)}, bf16[2,512,512]{2,1,0:T(8,128)(2,1)S(1)}) custom-call(bf16[128,512]{1,0:T(8,128)(2,1)S(1)} %copy-done.2, bf16[512,512]{1,0:T(8,128)(2,1)S(1)} %copy-done, bf16[512,512]{1,0:T(8,128)(2,1)S(1)} %copy-done.1, bf16[128,512]{1,0:T(8,128)(2,1)S(1)} %copy-done.3, s32[128,16]{1,0:T(8,128)S(1)} %copy.11.nb_ref, ...), custom_call_target="tpu_custom_call" | custom-call | tf_op jit(solution)/shard_map/sage_backward/pallas_call | solution.py:255
  77.9 1.6 %bitcast_convert_fusion = (f32[512,512]{1,0:T(8,128)}, f32[512,512]{1,0:T(8,128)}) fusion(bf16[2,512,512]{2,1,0:T(8,128)(2,1)S(1)} %get-tuple-element.6), kind=kLoop, calls=%fused_computation | loop fusion | flops 524288 | bytes 3145728 | tf_op jit(solution)/shard_map/convert_element_type | solution.py:294
  79.5 0.7 copy.13
Async XLA Ops:
  0.6 0.8 copy-start.5
  1.4 0.7 copy-start.4
  2.1 1.0 %copy-start = (bf16[512,512]{1,0:T(8,128)(2,1)S(1)}, bf16[512,512]{1,0:T(8,128)(2,1)}, u32[]{:S(2)}) copy-start(bf16[512,512]{1,0:T(8,128)(2,1)} %ws_ref.1) | copy-start | bytes 1572868
  3.1 1.0 %copy-start.1 = (bf16[512,512]{1,0:T(8,128)(2,1)S(1)}, bf16[512,512]{1,0:T(8,128)(2,1)}, u32[]{:S(2)}) copy-start(bf16[512,512]{1,0:T(8,128)(2,1)} %wn_ref.1) | copy-start | bytes 1572868
  4.2 0.9 %copy-start.2 = (bf16[128,512]{1,0:T(8,128)(2,1)S(1)}, bf16[128,512]{1,0:T(8,128)(2,1)}, u32[]{:S(2)}) copy-start(bf16[128,512]{1,0:T(8,128)(2,1)} %feat_ref.1) | copy-start | bytes 393220
  5.1 0.9 %copy-start.3 = (bf16[128,512]{1,0:T(8,128)(2,1)S(1)}, bf16[128,512]{1,0:T(8,128)(2,1)}, u32[]{:S(2)}) copy-start(bf16[128,512]{1,0:T(8,128)(2,1)} %cot_ref.1) | copy-start | bytes 393220

commit v2 on v1

v2 whole, which is shorter than its diff:
```python
import functools

import jax
import jax.numpy as jnp
from jax import lax
from jax.experimental import pallas as pl
from jax.experimental.pallas import tpu as pltpu
from jax.sharding import PartitionSpec as P

MESH = pl.DeviceIdType.MESH
F32 = jnp.float32
BF16 = jnp.bfloat16


def dot(left, right, left_dim=1, right_dim=0):
    return lax.dot_general(
        left, right, (((left_dim,), (right_dim,)), ((), ())), preferred_element_type=F32
    )


def iota(shape, dim):
    return lax.broadcasted_iota(jnp.int32, shape, dim)


def gelu_slope(v):
    root = 0.7978845608028654
    square = v * v
    t = jnp.tanh(root * (v + 0.044715 * square * v))
    return 0.5 * (1.0 + t) + (0.5 * root) * v * (1.0 - t * t) * (1.0 + 0.134145 * square)


def kernel(
    feat_hbm, ws_hbm, wn_hbm, cot_hbm, nb_hbm, rows_hbm, count_hbm,
    gfeat_ref, gw_ref,
    feat_ref, ws_ref, wn_ref, cot_ref, nb_ref, rows_ref, count_ref,
    sel_ref, adj_ref, adjt_ref, out_ref, halo_ref, back_ref, ret_ref,
    lt_ref, own_ref, pair_out, pair_in, one_out, one_in, two_out, two_in, y_ref, base_ref,
    load_sem, a2a_send, a2a_recv, pair_send, pair_recv, one_send, one_recv, two_send, two_recv,
    y_send, y_recv, ag1_send, ag1_recv, ag2_send, ag2_recv, fin_send, fin_recv,
):
    grp = lax.axis_index("grp")
    dom = lax.axis_index("dom")
    core = lax.rem(dom, 2)
    y = lax.rem(dom // 2, 8)
    x = dom // 16
    other = 1 - core
    sibling = {"dom": dom + 1 - 2 * core}

    def at_x(i):
        return {"dom": i * 16 + y * 2 + core}

    def at_y(i):
        return {"dom": x * 16 + i * 2 + core}

    def at_z(i):
        return {"grp": i}

    def dom_peer(r):
        return lax.rem(dom + r, 64)

    def loop(first, last, body):
        lax.fori_loop(first, last, lambda i, c: (body(i), c)[1], 0)

    def remote(src, dst, send, recv, device):
        return pltpu.make_async_remote_copy(
            src_ref=src, dst_ref=dst, send_sem=send, recv_sem=recv,
            device_id=device, device_id_type=MESH,
        )

    def wait(ref, sem):
        pltpu.make_async_copy(ref, ref, sem).wait()

    def part(i, size):
        return pl.ds(pl.multiple_of(i * size, size), size)

    loads = [
        pltpu.make_async_copy(src, dst, load_sem.at[i])
        for i, (src, dst) in enumerate([
            (rows_hbm, rows_ref), (count_hbm, count_ref), (feat_hbm, feat_ref), (nb_hbm, nb_ref),
            (ws_hbm, ws_ref), (wn_hbm, wn_ref), (cot_hbm, cot_ref),
        ])
    ]
    for load in loads:
        load.start()

    barrier = pltpu.get_barrier_semaphore()
    loop(1, 64, lambda r: pl.semaphore_signal(
        barrier, inc=1, device_id={"dom": dom_peer(r)}, device_id_type=MESH))
    loop(1, 8, lambda r: pl.semaphore_signal(
        barrier, inc=1, device_id=at_z(lax.rem(grp + r, 8)), device_id_type=MESH))

    col = iota((1, 1024), 1)
    slot_of = jnp.bitwise_and(col, 7)
    half_of = jnp.bitwise_and(lax.shift_right_logical(col, 3), 1)
    in_peer = (iota((64, 1024), 0) == lax.shift_right_logical(col, 4)).astype(BF16)
    for load in loads[:3]:
        load.wait()
    counts = jnp.broadcast_to(count_ref[...], (8, 64))
    table = jnp.concatenate([rows_ref[...], counts], axis=0).astype(F32).astype(BF16)
    spread = dot(table, in_peer)
    row = jnp.sum(jnp.where(iota((8, 1024), 0) == slot_of, spread[0:8], 0.0), axis=0, keepdims=True)
    live = spread[8:9] > slot_of.astype(F32)
    target = jnp.where(live, row + 128.0 * half_of.astype(F32), 512.0)
    sel_ref[...] = (iota((256, 1024), 0).astype(F32) == target).astype(BF16)
    feat = feat_ref[...]
    feat2 = jnp.concatenate([feat[:, :256], feat[:, 256:]], axis=0)
    out_ref[...] = dot(sel_ref[...], feat2, 0, 0).astype(BF16)

    pl.semaphore_wait(barrier, 70)

    def send_boundary(src, dst, k):
        def one(r):
            peer = dom_peer(r)
            remote(src.at[part(peer, 16)], dst.at[part(dom, 16)], a2a_send.at[k], a2a_recv.at[k],
                   {"dom": peer}).start()
        loop(1, 64, one)
        dst[part(dom, 16), :] = src[part(dom, 16), :]

    def wait_boundary(dst, k):
        wait(dst.at[pl.ds(0, 63 * 16)], a2a_recv.at[k])

    send_boundary(out_ref, halo_ref, 0)

    loads[3].wait()
    nb = nb_ref[...]
    entry = nb - 128
    place_of = lax.shift_left(lax.shift_right_arithmetic(entry, 3), 4) + jnp.bitwise_and(entry, 7)
    row_ids = iota((1024, 128), 0)
    count = jnp.zeros((1024, 128), F32)
    for k in range(8, 16):
        count = count + jnp.where(row_ids == place_of[k:k + 1, :], 1.0, 0.0)
    lower = count.T
    adjt_ref[:, 0:128] = count.astype(BF16)
    adjt_ref[:, 128:256] = pltpu.roll(count, 8, 0).astype(BF16)
    adj_ref[0:128, :] = lower.astype(BF16)
    adj_ref[128:256, :] = pltpu.roll(lower, 8, 1).astype(BF16)
    own_ids = iota((128, 128), 0)
    own_t = jnp.zeros((128, 128), F32)
    for k in range(8):
        own_t = own_t + jnp.where(own_ids == nb[k:k + 1, :], 1.0, 0.0)
    own_adj = own_t.T.astype(BF16)
    own_adj_t = own_t.astype(BF16)
    own_sum = dot(own_adj, feat)
    lt_ref[0] = feat.astype(F32).T.astype(BF16)
    for load in loads[4:]:
        load.wait()
    pre_self = dot(feat, ws_ref[...])

    wait_boundary(halo_ref, 0)
    halo_sum = dot(adj_ref[...], halo_ref[...])
    summed = own_sum + jnp.concatenate([halo_sum[0:128], halo_sum[128:256]], axis=1)
    agg = (summed * (1.0 / 16.0)).astype(BF16)
    pre = pre_self + dot(agg, wn_ref[...])
    grad_pre = (cot_ref[...].astype(F32) * gelu_slope(pre)).astype(BF16)

    lt_ref[1] = agg.astype(F32).T.astype(BF16)
    scale = 65536.0 ** -0.5
    pair_out[...] = (dot(lt_ref[other], grad_pre) * scale).astype(BF16)

    def send_pair(first):
        def one(r):
            i = lax.rem(first + r, 8)
            remote(pair_out.at[part(i, 64)], pair_in.at[part(i, 64)], pair_send.at[i],
                   pair_recv.at[i], sibling).start()
        loop(0, 8, one)

    send_pair(lax.rem(core * (grp + 1) + other * (x * 2 + 2), 8))
    own_ref[...] = dot(lt_ref[core], grad_pre) * scale

    grad_agg = (dot(grad_pre, wn_ref[...], 1, 1) * (1.0 / 16.0)).astype(BF16)
    grad_agg2 = jnp.concatenate([grad_agg[:, :256], grad_agg[:, 256:]], axis=0)
    back_ref[...] = dot(adjt_ref[...], grad_agg2).astype(BF16)

    def features_gradient():
        wait_boundary(ret_ref, 1)
        returned = dot(sel_ref[...], ret_ref[...])
        gfeat_ref[...] = (
            base_ref[...] + jnp.concatenate([returned[0:128], returned[128:256]], axis=1)
        ).astype(BF16)

    def sum_matrix(c, n1, me1, at1, n2, me2, at2):
        rows1 = 512 // n1
        rows2 = rows1 // n2

        def send_first(r):
            i = lax.rem(me1 + r, n1)
            for j in range(rows1 // 64):
                piece = i * (rows1 // 64) + j
                wait(pair_in.at[part(piece, 64)], pair_recv.at[piece])
            rows = part(i, rows1)
            one_out[rows, :] = (own_ref[rows, :] + pair_in[rows, :].astype(F32)).astype(BF16)
            remote(one_out.at[rows], one_in.at[part(me1, rows1)], one_send, one_recv, at1(i)).start()
        loop(1, n1, send_first)

        send_boundary(back_ref, ret_ref, 1)
        base_ref[...] = dot(grad_pre, ws_ref[...], 1, 1) + dot(own_adj_t, grad_agg)

        for j in range(rows1 // 64):
            piece = me1 * (rows1 // 64) + j
            wait(pair_in.at[part(piece, 64)], pair_recv.at[piece])
        mine = part(me1, rows1)
        total = own_ref[mine, :] + pair_in[mine, :].astype(F32)
        wait(one_in.at[pl.ds(0, 512 - rows1)], one_recv)
        for r in range(1, n1):
            total = total + one_in[part(lax.rem(me1 + r, n1), rows1), :].astype(F32)

        own_ref[0:rows1, :] = total
        two_out[0:rows1, :] = total.astype(BF16)

        def send_second(r):
            i = lax.rem(me2 + r, n2)
            remote(two_out.at[part(i, rows2)], two_in.at[part(me2, rows2)], two_send, two_recv,
                   at2(i)).start()
        loop(1, n2, send_second)
        wait(two_in.at[pl.ds(0, rows1 - rows2)], two_recv)
        small = own_ref[part(me2, rows2), :]
        for r in range(1, n2):
            small = small + two_in[part(lax.rem(me2 + r, n2), rows2), :].astype(F32)

        y_ref[part(y, 16), :] = small.astype(BF16)

        def send_y(r):
            remote(y_ref.at[part(y, 16)], y_ref.at[part(y, 16)], y_send, y_recv,
                   at_y(lax.rem(y + r, 8))).start()
        loop(1, 8, send_y)
        wait(y_ref.at[pl.ds(0, 7 * 16)], y_recv)
        done = y_ref[0:16, :].astype(F32)
        for i in range(1, 8):
            done = done + y_ref[16 * i:16 * i + 16, :].astype(F32)
        at_two = pl.ds(pl.multiple_of(me1 * rows1 + me2 * rows2, rows2), rows2)
        gw_ref[c, at_two, :] = done.astype(BF16)

        def gather_two(r):
            remote(gw_ref.at[c, at_two], gw_ref.at[c, at_two], ag1_send, ag1_recv,
                   at2(lax.rem(me2 + r, n2))).start()
        loop(1, n2, gather_two)
        features_gradient()
        wait(gw_ref.at[c, pl.ds(0, rows1 - rows2)], ag1_recv)

        def gather_one(r):
            remote(gw_ref.at[c, mine], gw_ref.at[c, mine], ag2_send, ag2_recv.at[me1],
                   at1(lax.rem(me1 + r, n1))).start()
        loop(1, n1, gather_one)

        def forward(i):
            for j in range(rows1 // 64):
                piece = i * (rows1 // 64) + j
                rows = part(piece, 64)
                remote(gw_ref.at[c, rows], gw_ref.at[c, rows], fin_send.at[piece],
                       fin_recv.at[piece], sibling).start()
        forward(me1)

        def arrived(r):
            i = lax.rem(me1 + r, n1)
            wait(gw_ref.at[c, part(i, rows1)], ag2_recv.at[i])
            forward(i)
        loop(1, n1, arrived)

        wait(one_out.at[pl.ds(0, 512 - rows1)], one_send)
        wait(two_out.at[pl.ds(0, rows1 - rows2)], two_send)
        wait(gw_ref.at[c, pl.ds(0, rows1 - rows2)], ag1_send)
        wait(gw_ref.at[c, pl.ds(0, 512 - rows1)], ag2_send)

    @pl.when(core == 0)
    def _():
        sum_matrix(0, 8, grp, at_z, 4, x, at_x)

    @pl.when(core == 1)
    def _():
        sum_matrix(1, 4, x, at_x, 8, grp, at_z)

    wait(out_ref.at[pl.ds(0, 63 * 16)], a2a_send.at[0])
    wait(back_ref.at[pl.ds(0, 63 * 16)], a2a_send.at[1])
    wait(y_ref.at[pl.ds(0, 7 * 16)], y_send)

    def finish(i):
        wait(pair_out.at[part(i, 64)], pair_send.at[i])
        wait(gw_ref.at[core, part(i, 64)], fin_send.at[i])
        wait(gw_ref.at[other, part(i, 64)], fin_recv.at[i])
    loop(0, 8, finish)


def write_kernel(gfeat_in, gw_in, gfeat_ref, gws_ref, gwn_ref, wide_ref, sem):
    copies = [pltpu.make_async_copy(gfeat_in, gfeat_ref, sem.at[0])]
    copies[0].start()
    for c, ref in enumerate((gws_ref, gwn_ref)):
        for half in range(2):
            rows = pl.ds(256 * half, 256)
            wide_ref[c, rows, :] = gw_in[c, rows, :].astype(F32)
            copy = pltpu.make_async_copy(
                wide_ref.at[c, rows], ref.at[rows], sem.at[1 + 2 * c + half])
            copy.start()
            copies.append(copy)
    for copy in copies:
        copy.wait()


def local(features, w_self, w_neigh, cotangent, neighbors, send_rows, send_count):
    vmem = pl.BlockSpec(memory_space=pltpu.VMEM)
    hbm = pl.BlockSpec(memory_space=pltpu.HBM)
    dma = pltpu.SemaphoreType.DMA
    grad_features, grads = pl.pallas_call(
        kernel,
        out_shape=(
            pltpu.VMEM((128, 512), BF16),
            pltpu.VMEM((2, 512, 512), BF16),
        ),
        in_specs=[hbm] * 7,
        out_specs=(vmem, vmem),
        scratch_shapes=[
            pltpu.VMEM((128, 512), BF16),
            pltpu.VMEM((512, 512), BF16),
            pltpu.VMEM((512, 512), BF16),
            pltpu.VMEM((128, 512), BF16),
            pltpu.VMEM((16, 128), jnp.int32),
            pltpu.VMEM((8, 64), jnp.int32),
            pltpu.VMEM((1, 64), jnp.int32),
            pltpu.VMEM((256, 1024), BF16),
            pltpu.VMEM((256, 1024), BF16),
            pltpu.VMEM((1024, 256), BF16),
            pltpu.VMEM((1024, 256), BF16),
            pltpu.VMEM((1024, 256), BF16),
            pltpu.VMEM((1024, 256), BF16),
            pltpu.VMEM((1024, 256), BF16),
            pltpu.VMEM((2, 512, 128), BF16),
            pltpu.VMEM((512, 512), F32),
            pltpu.VMEM((512, 512), BF16),
            pltpu.VMEM((512, 512), BF16),
            pltpu.VMEM((512, 512), BF16),
            pltpu.VMEM((512, 512), BF16),
            pltpu.VMEM((128, 512), BF16),
            pltpu.VMEM((128, 512), BF16),
            pltpu.VMEM((128, 512), BF16),
            pltpu.VMEM((128, 512), F32),
            dma((7,)), dma((2,)), dma((2,)), dma((8,)), dma((8,)), dma, dma, dma, dma,
            dma, dma, dma, dma, dma, dma((8,)), dma((8,)), dma((8,)),
        ],
        compiler_params=pltpu.CompilerParams(
            collective_id=0, has_side_effects=True, vmem_limit_bytes=40 << 20
        ),
        name="sage_backward",
    )(*(
        pltpu.with_memory_space_constraint(array, pltpu.HBM)
        for array in (
            features, w_self, w_neigh, cotangent, neighbors.T,
            send_rows.reshape(64, 8).T, send_count.reshape(1, 64),
        )
    ))
    return pl.pallas_call(
        write_kernel,
        out_shape=(
            jax.ShapeDtypeStruct((128, 512), BF16),
            jax.ShapeDtypeStruct((512, 512), F32),
            jax.ShapeDtypeStruct((512, 512), F32),
        ),
        in_specs=[vmem, vmem],
        out_specs=(hbm, hbm, hbm),
        scratch_shapes=[pltpu.VMEM((2, 512, 512), F32), dma((5,))],
        compiler_params=pltpu.CompilerParams(vmem_limit_bytes=8 << 20),
        name="write_results",
    )(grad_features, grads)


def solution(mesh):
    placed = (
        P(("grp", "dom"), None),
        P(),
        P(),
        P(("grp", "dom"), None),
        P(("grp", "dom"), None),
        P("grp", "dom", None, None),
        P("grp", "dom", None),
    )
    return jax.shard_map(
        local,
        mesh=mesh,
        in_specs=placed,
        out_specs=(P(("grp", "dom"), None), P(), P()),
        check_vma=False,
    )
```

time: 80.4 us -> 71.9 us (0.89)
  local copies, waits for them, and re-layouts: 5.97 us -> 0 us
  other arithmetic: 1.6 us -> 0 us
    unnamed x15 -> x0, local copies, waits for them, and re-layouts: 5.97 us -> none
    convert_element_type x1 -> x0, other arithmetic: 1.6 us -> none  [local(): return (grad_features, grads[0].astype(F32), grads[1].astype(F32))]
    pallas_call x1 -> x2, Pallas kernels: 71.9 us -> 71.2 us  [the longest x1 69.8 us: local(): pl.pallas_call(kernel, out_shape=(pltpu.VMEM((128, 512), BF16), pltpu.VME...]
where the time goes in v2:
time: 71.9 us; the launch traced here: 71.8 us
  Pallas kernels  71.2 us (99%)
    pallas_call x1, Pallas kernels, local(): pl.pallas_call(kernel, out_shape=(pltpu.VMEM((128, 512), BF16), pltpu.VME...  69.8 us

profile of v2, /device:TPU:1, one launch (start us, length us, event | category | flops | bytes accessed | tf_op | source)
XLA Modules:
  0.0 71.8 jit_solution(15083955529632335946)
XLA Ops:
  0.6 69.8 %sage_backward.1 = (bf16[128,512]{1,0:T(8,128)(2,1)S(1)}, bf16[2,512,512]{2,1,0:T(8,128)(2,1)S(1)}) custom-call(bf16[128,512]{1,0:T(8,128)(2,1)} %feat_hbm.1, bf16[512,512]{1,0:T(8,128)(2,1)} %ws_hbm.1, bf16[512,512]{1,0:T(8,128)(2,1)} %wn_hbm.1, bf16[128,512]{1,0:T(8,128)(2,1)} %cot_hbm.1, s32[16,128]{1,0:T(8,128)} %bitcast.5, s32[8,64]{1,0:T(8,128)} %bitcast.6, ...), custom_call_target="tpu_custom_call" | custom-call | tf_op jit(solution)/shard_map/sage_backward/pallas_call | solution.py:302
  70.4 1.4 %write_results.1 = (bf16[128,512]{1,0:T(8,128)(2,1)}, f32[512,512]{1,0:T(8,128)}, f32[512,512]{1,0:T(8,128)}) custom-call(bf16[128,512]{1,0:T(8,128)(2,1)S(1)} %get-tuple-element.5.gfeat_in, bf16[2,512,512]{2,1,0:T(8,128)(2,1)S(1)} %get-tuple-element.6.gw_in), custom_call_target="tpu_custom_call" | custom-call | tf_op jit(solution)/shard_map/write_results/pallas_call | solution.py:349

commit v3 on v2

v3 whole, which is shorter than its diff:
```python
import functools

import jax
import jax.numpy as jnp
from jax import lax
from jax.experimental import pallas as pl
from jax.experimental.pallas import tpu as pltpu
from jax.sharding import PartitionSpec as P

MESH = pl.DeviceIdType.MESH
F32 = jnp.float32
BF16 = jnp.bfloat16


STRIPS = ((0, 256, "xzy"), (256, 128, "zxy"), (384, 128, "yxz"))
BATCHES = (((1, 16, 1),), ((16, 32, 1),), ((32, 48, 1),), ((48, 64, 1),))


def dot(left, right, left_dim=1, right_dim=0):
    return lax.dot_general(
        left, right, (((left_dim,), (right_dim,)), ((), ())), preferred_element_type=F32
    )


def iota(shape, dim):
    return lax.broadcasted_iota(jnp.int32, shape, dim)


def gelu_slope(v):
    root = 0.7978845608028654
    square = v * v
    t = jnp.tanh(root * (v + 0.044715 * square * v))
    return 0.5 * (1.0 + t) + (0.5 * root) * v * (1.0 - t * t) * (1.0 + 0.134145 * square)


def kernel(
    feat_hbm, ws_hbm, wn_hbm, cot_hbm, nb_hbm, rows_hbm, count_hbm,
    gfeat_ref, gw_ref,
    feat_ref, ws_ref, wn_ref, cot_ref, nb_ref, rows_ref, count_ref,
    sel_ref, adj_ref, adjt_ref, out_ref, halo_ref, back_ref, ret_ref,
    lt_ref, own_ref, pair_out, pair_in, one_out, one_in, sum_ref, two_out, two_in, three_ref, base_ref,
    load_sem, a2a_send, a2a_recv, pair_send, pair_recv, one_send, one_recv, two_send, two_recv,
    three_send, three_recv, ag1_send, ag1_recv, ag2_send, ag2_recv, fin_send, fin_recv,
):
    grp = lax.axis_index("grp")
    dom = lax.axis_index("dom")
    core = lax.rem(dom, 2)
    other = 1 - core
    sibling = {"dom": dom + 1 - 2 * core}
    y = lax.rem(dom // 2, 8)
    x = dom // 16

    axis_x = (4, x, lambda i: {"dom": i * 16 + y * 2 + core})
    axis_y = (8, y, lambda i: {"dom": x * 16 + i * 2 + core})
    axis_z = (8, grp, lambda i: {"grp": i})
    axes = {"x": axis_x, "y": axis_y, "z": axis_z}
    strips = tuple(
        (first, width) + tuple(axes[name] for name in order) for first, width, order in STRIPS
    )

    def dom_peer(r):
        return lax.rem(dom + r, 64)

    def loop(first, last, body):
        lax.fori_loop(first, last, lambda i, c: (body(i), c)[1], 0)

    def remote(src, dst, send, recv, device):
        return pltpu.make_async_remote_copy(
            src_ref=src, dst_ref=dst, send_sem=send, recv_sem=recv,
            device_id=device, device_id_type=MESH,
        )

    def wait(ref, sem):
        pltpu.make_async_copy(ref, ref, sem).wait()

    def part(i, size):
        return pl.ds(pl.multiple_of(i * size, size), size)

    loads = [
        pltpu.make_async_copy(src, dst, load_sem.at[i])
        for i, (src, dst) in enumerate([
            (rows_hbm, rows_ref), (count_hbm, count_ref), (feat_hbm, feat_ref), (nb_hbm, nb_ref),
            (ws_hbm, ws_ref), (wn_hbm, wn_ref), (cot_hbm, cot_ref),
        ])
    ]
    for load in loads:
        load.start()

    barrier = pltpu.get_barrier_semaphore()
    with jax.named_scope("greet"):
        loop(1, 64, lambda r: pl.semaphore_signal(
            barrier, inc=1, device_id={"dom": dom_peer(r)}, device_id_type=MESH))
        loop(1, 8, lambda r: pl.semaphore_signal(
            barrier, inc=1, device_id={"grp": lax.rem(grp + r, 8)}, device_id_type=MESH))

    with jax.named_scope("outgoing"):
        col = iota((1, 1024), 1)
        slot_of = jnp.bitwise_and(col, 7)
        half_of = jnp.bitwise_and(lax.shift_right_logical(col, 3), 1)
        in_peer = (iota((64, 1024), 0) == lax.shift_right_logical(col, 4)).astype(BF16)
        for load in loads[:3]:
            load.wait()
        counts = jnp.broadcast_to(count_ref[...], (8, 64))
        table = jnp.concatenate([rows_ref[...], counts], axis=0).astype(F32).astype(BF16)
        spread = dot(table, in_peer)
        row = jnp.sum(
            jnp.where(iota((8, 1024), 0) == slot_of, spread[0:8], 0.0), axis=0, keepdims=True)
        live = spread[8:9] > slot_of.astype(F32)
        target = jnp.where(live, row + 128.0 * half_of.astype(F32), 512.0)
        sel_ref[...] = (iota((256, 1024), 0).astype(F32) == target).astype(BF16)
        feat = feat_ref[...]
        feat2 = jnp.concatenate([feat[:, :256], feat[:, 256:]], axis=0)
        out_ref[...] = dot(sel_ref[...], feat2, 0, 0).astype(BF16)

    with jax.named_scope("barrier"):
        pl.semaphore_wait(barrier, 70)

    def send_boundary(src, dst, k, *distances):
        def one(r):
            peer = dom_peer(r)
            remote(src.at[part(peer, 16)], dst.at[part(dom, 16)], a2a_send.at[k], a2a_recv.at[k],
                   {"dom": peer}).start()
        for first, last, step in distances:
            loop(0, (last - first) // step, lambda i: one(first + step * i))

    def keep_boundary(src, dst):
        dst[part(dom, 16), :] = src[part(dom, 16), :]

    def wait_boundary(dst, k):
        wait(dst.at[pl.ds(0, 63 * 16)], a2a_recv.at[k])

    with jax.named_scope("send_rows"):
        send_boundary(out_ref, halo_ref, 0, (1, 64, 1))
        keep_boundary(out_ref, halo_ref)

    with jax.named_scope("adjacency"):
        loads[3].wait()
        nb = nb_ref[...]
        entry = nb - 128
        place_of = (
            lax.shift_left(lax.shift_right_arithmetic(entry, 3), 4) + jnp.bitwise_and(entry, 7))
        row_ids = iota((1024, 128), 0)
        count = jnp.zeros((1024, 128), F32)
        for k in range(8, 16):
            count = count + jnp.where(row_ids == place_of[k:k + 1, :], 1.0, 0.0)
        lower = count.T
        adjt_ref[:, 0:128] = count.astype(BF16)
        adjt_ref[:, 128:256] = pltpu.roll(count, 8, 0).astype(BF16)
        adj_ref[0:128, :] = lower.astype(BF16)
        adj_ref[128:256, :] = pltpu.roll(lower, 8, 1).astype(BF16)
        own_ids = iota((128, 128), 0)
        own_t = jnp.zeros((128, 128), F32)
        for k in range(8):
            own_t = own_t + jnp.where(own_ids == nb[k:k + 1, :], 1.0, 0.0)
        own_adj = own_t.T.astype(BF16)
        own_adj_t = own_t.astype(BF16)
        own_sum = dot(own_adj, feat)
        lt_ref[0] = feat.astype(F32).T.astype(BF16)
        for load in loads[4:]:
            load.wait()
        pre_self = dot(feat, ws_ref[...])

    with jax.named_scope("wait_rows"):
        wait_boundary(halo_ref, 0)
    with jax.named_scope("grad_pre"):
        halo_sum = dot(adj_ref[...], halo_ref[...])
        summed = own_sum + jnp.concatenate([halo_sum[0:128], halo_sum[128:256]], axis=1)
        agg = (summed * (1.0 / 16.0)).astype(BF16)
        pre = pre_self + dot(agg, wn_ref[...])
        grad_pre = (cot_ref[...].astype(F32) * gelu_slope(pre)).astype(BF16)

    with jax.named_scope("weight_grads"):
        lt_ref[1] = agg.astype(F32).T.astype(BF16)
        scale = 65536.0 ** -0.5
        pair_out[...] = (dot(lt_ref[other], grad_pre) * scale).astype(BF16)
        for r in range(4):
            i = lax.rem(x + 1 + r, 4)
            remote(pair_out.at[part(i, 128)], pair_in.at[part(i, 128)], pair_send.at[i],
                   pair_recv.at[i], sibling).start()
        own_ref[...] = dot(lt_ref[core], grad_pre) * scale

    with jax.named_scope("boundary_grads"):
        grad_agg = (dot(grad_pre, wn_ref[...], 1, 1) * (1.0 / 16.0)).astype(BF16)
        grad_agg2 = jnp.concatenate([grad_agg[:, :256], grad_agg[:, 256:]], axis=0)
        back_ref[...] = dot(adjt_ref[...], grad_agg2).astype(BF16)

    def send_one(s, i):
        first, width, (n, me, at), _, _ = strips[s]
        rows = part(i, 512 // n)
        cols = pl.ds(first, width)
        one_out[s][rows, :] = (
            own_ref[rows, cols] + pair_in[rows, cols].astype(F32)).astype(BF16)

        @pl.when(i != me)
        def _():
            remote(one_out[s].at[rows], one_in[s].at[part(me, 512 // n)], one_send.at[s],
                   one_recv.at[s], at(i)).start()

    with jax.named_scope("step_one"):
        for r in range(4):
            i = lax.rem(x + 1 + r, 4)
            wait(pair_in.at[part(i, 128)], pair_recv.at[i])
            for s, (_, _, (n1, _, _), _, _) in enumerate(strips):
                for j in range(n1 // 4):
                    send_one(s, n1 // 4 * i + j)

    with jax.named_scope("send_grads"):
        send_boundary(back_ref, ret_ref, 1, *BATCHES[0])
        keep_boundary(back_ref, ret_ref)
    with jax.named_scope("base"):
        base_ref[...] = dot(grad_pre, ws_ref[...], 1, 1) + dot(own_adj_t, grad_agg)

    for s, (first, width, (n1, me1, _), (n2, me2, at2), _) in enumerate(strips):
        with jax.named_scope("step_two_%d" % s):
            rows1 = 512 // n1
            mine = part(me1, rows1)
            cols = pl.ds(first, width)
            total = own_ref[mine, cols] + pair_in[mine, cols].astype(F32)
            wait(one_in[s].at[pl.ds(0, 512 - rows1)], one_recv.at[s])
            for r in range(1, n1):
                total = total + one_in[s][part(lax.rem(me1 + r, n1), rows1), :].astype(F32)
            sum_ref[s][...] = total
            two_out[s][...] = total.astype(BF16)
            for r in range(1, n2):
                i = lax.rem(me2 + r, n2)
                remote(two_out[s].at[part(i, 16)], two_in[s].at[part(me2, 16)], two_send.at[s],
                       two_recv.at[s], at2(i)).start()

    send_boundary(back_ref, ret_ref, 1, *BATCHES[1])

    for s, (_, _, _, (n2, me2, _), (n3, me3, at3)) in enumerate(strips):
        with jax.named_scope("step_three_%d" % s):
            small = sum_ref[s][part(me2, 16), :]
            wait(two_in[s].at[pl.ds(0, 16 * (n2 - 1))], two_recv.at[s])
            for r in range(1, n2):
                small = small + two_in[s][part(lax.rem(me2 + r, n2), 16), :].astype(F32)
            three_ref[s][part(me3, 16), :] = small.astype(BF16)
            for r in range(1, n3):
                here = three_ref[s].at[part(me3, 16)]
                remote(here, here, three_send.at[s], three_recv.at[s],
                       at3(lax.rem(me3 + r, n3))).start()

    send_boundary(back_ref, ret_ref, 1, *BATCHES[2])

    def final(s, rows, count):
        first, width = strips[s][:2]
        return gw_ref.at[core, pl.ds(rows, count), pl.ds(first, width)]

    for s, (first, width, (n1, me1, _), (n2, me2, at2), (n3, _, _)) in enumerate(strips):
        with jax.named_scope("gather_one_%d" % s):
            wait(three_ref[s].at[pl.ds(0, 16 * (n3 - 1))], three_recv.at[s])
            done = three_ref[s][0:16, :].astype(F32)
            for i in range(1, n3):
                done = done + three_ref[s][16 * i:16 * i + 16, :].astype(F32)
            row = pl.multiple_of(me1 * (512 // n1) + me2 * 16, 16)
            gw_ref[core, pl.ds(row, 16), pl.ds(first, width)] = done.astype(BF16)
            for r in range(1, n2):
                remote(final(s, row, 16), final(s, row, 16), ag1_send.at[s], ag1_recv.at[s],
                       at2(lax.rem(me2 + r, n2))).start()

    send_boundary(back_ref, ret_ref, 1, *BATCHES[3])

    def forward(s, unit, row, count):
        remote(final(s, row, count), final(s, row, count), fin_send.at[s, unit],
               fin_recv.at[s, unit], sibling).start()

    for s, (_, _, (n1, me1, at1), (n2, _, _), _) in enumerate(strips):
        with jax.named_scope("gather_two_%d" % s):
            rows1 = 512 // n1
            wait(final(s, 0, 16 * (n2 - 1)), ag1_recv.at[s])
            row = pl.multiple_of(me1 * rows1, rows1)
            for r in range(1, n1):
                unit = me1 if n1 == 4 else 0
                remote(final(s, row, rows1), final(s, row, rows1), ag2_send.at[s],
                       ag2_recv.at[s, unit], at1(lax.rem(me1 + r, n1))).start()
            if n1 == 4:
                forward(s, me1, row, rows1)
    with jax.named_scope("forward"):
        for s, (_, _, (n1, me1, _), _, _) in enumerate(strips):
            if n1 == 4:
                for r in range(1, 4):
                    i = lax.rem(me1 + r, 4)
                    row = pl.multiple_of(i * 128, 128)
                    wait(final(s, row, 128), ag2_recv.at[s, i])
                    forward(s, i, row, 128)
            else:
                wait(final(s, 0, 448), ag2_recv.at[s, 0])
                forward(s, 0, 0, 512)

    with jax.named_scope("wait_grads"):
        wait_boundary(ret_ref, 1)
    with jax.named_scope("feature_grads"):
        returned = dot(sel_ref[...], ret_ref[...])
        gfeat_ref[...] = (
            base_ref[...] + jnp.concatenate([returned[0:128], returned[128:256]], axis=1)
        ).astype(BF16)

    with jax.named_scope("finish"):
        wait(out_ref.at[pl.ds(0, 63 * 16)], a2a_send.at[0])
        wait(back_ref.at[pl.ds(0, 63 * 16)], a2a_send.at[1])
        for i in range(4):
            wait(pair_out.at[pl.ds(128 * i, 128)], pair_send.at[i])
        for s, (_, _, (n1, _, _), (n2, _, _), (n3, _, _)) in enumerate(strips):
            rows1 = 512 // n1
            wait(one_out[s].at[pl.ds(0, 512 - rows1)], one_send.at[s])
            wait(two_out[s].at[pl.ds(0, 16 * (n2 - 1))], two_send.at[s])
            wait(three_ref[s].at[pl.ds(0, 16 * (n3 - 1))], three_send.at[s])
            wait(final(s, 0, 16 * (n2 - 1)), ag1_send.at[s])
            wait(final(s, 0, 512 - rows1), ag2_send.at[s])
            units = 4 if n1 == 4 else 1
            for unit in range(units):
                wait(final(s, 0, 512 // units), fin_send.at[s, unit])
                wait(final(s, 0, 512 // units), fin_recv.at[s, unit])


def write_kernel(gfeat_in, gw_in, gfeat_ref, gws_ref, gwn_ref, wide_ref, sem):
    copies = [pltpu.make_async_copy(gfeat_in, gfeat_ref, sem.at[0])]
    copies[0].start()
    for c, ref in enumerate((gws_ref, gwn_ref)):
        for half in range(2):
            rows = pl.ds(256 * half, 256)
            wide_ref[c, rows, :] = gw_in[c, rows, :].astype(F32)
            copy = pltpu.make_async_copy(
                wide_ref.at[c, rows], ref.at[rows], sem.at[1 + 2 * c + half])
            copy.start()
            copies.append(copy)
    for copy in copies:
        copy.wait()


def strip_scratch(shape, dtype):
    return tuple(
        pltpu.VMEM(shape(width, 4 if order[0] == "x" else 8), dtype) for _, width, order in STRIPS
    )


def local(features, w_self, w_neigh, cotangent, neighbors, send_rows, send_count):
    vmem = pl.BlockSpec(memory_space=pltpu.VMEM)
    hbm = pl.BlockSpec(memory_space=pltpu.HBM)
    dma = pltpu.SemaphoreType.DMA
    grad_features, grads = pl.pallas_call(
        kernel,
        out_shape=(
            pltpu.VMEM((128, 512), BF16),
            pltpu.VMEM((2, 512, 512), BF16),
        ),
        in_specs=[hbm] * 7,
        out_specs=(vmem, vmem),
        scratch_shapes=[
            pltpu.VMEM((128, 512), BF16),
            pltpu.VMEM((512, 512), BF16),
            pltpu.VMEM((512, 512), BF16),
            pltpu.VMEM((128, 512), BF16),
            pltpu.VMEM((16, 128), jnp.int32),
            pltpu.VMEM((8, 64), jnp.int32),
            pltpu.VMEM((1, 64), jnp.int32),
            pltpu.VMEM((256, 1024), BF16),
            pltpu.VMEM((256, 1024), BF16),
            pltpu.VMEM((1024, 256), BF16),
            pltpu.VMEM((1024, 256), BF16),
            pltpu.VMEM((1024, 256), BF16),
            pltpu.VMEM((1024, 256), BF16),
            pltpu.VMEM((1024, 256), BF16),
            pltpu.VMEM((2, 512, 128), BF16),
            pltpu.VMEM((512, 512), F32),
            pltpu.VMEM((512, 512), BF16),
            pltpu.VMEM((512, 512), BF16),
            strip_scratch(lambda w, n: (512, w), BF16),
            strip_scratch(lambda w, n: (512, w), BF16),
            strip_scratch(lambda w, n: (512 // n, w), F32),
            strip_scratch(lambda w, n: (512 // n, w), BF16),
            strip_scratch(lambda w, n: (512 // n, w), BF16),
            strip_scratch(lambda w, n: (128, w), BF16),
            pltpu.VMEM((128, 512), F32),
            dma((7,)), dma((2,)), dma((2,)), dma((4,)), dma((4,)),
            *([dma((len(STRIPS),))] * 9), *([dma((len(STRIPS), 4))] * 3),
        ],
        compiler_params=pltpu.CompilerParams(
            collective_id=0, has_side_effects=True, vmem_limit_bytes=40 << 20
        ),
        name="sage_backward",
    )(*(
        pltpu.with_memory_space_constraint(array, pltpu.HBM)
        for array in (
            features, w_self, w_neigh, cotangent, neighbors.T,
            send_rows.reshape(64, 8).T, send_count.reshape(1, 64),
        )
    ))
    return pl.pallas_call(
        write_kernel,
        out_shape=(
            jax.ShapeDtypeStruct((128, 512), BF16),
            jax.ShapeDtypeStruct((512, 512), F32),
            jax.ShapeDtypeStruct((512, 512), F32),
        ),
        in_specs=[vmem, vmem],
        out_specs=(hbm, hbm, hbm),
        scratch_shapes=[pltpu.VMEM((2, 512, 512), F32), dma((5,))],
        compiler_params=pltpu.CompilerParams(vmem_limit_bytes=8 << 20),
        name="write_results",
    )(grad_features, grads)


def solution(mesh):
    placed = (
        P(("grp", "dom"), None),
        P(),
        P(),
        P(("grp", "dom"), None),
        P(("grp", "dom"), None),
        P("grp", "dom", None, None),
        P("grp", "dom", None),
    )
    return jax.shard_map(
        local,
        mesh=mesh,
        in_specs=placed,
        out_specs=(P(("grp", "dom"), None), P(), P()),
        check_vma=False,
    )
```

time: 71.9 us -> 66.7 us (0.928)
  Pallas kernels: 71.2 us -> 66 us
    pallas_call x1, Pallas kernels: 69.8 us -> 64.6 us  [local(): pl.pallas_call(kernel, out_shape=(pltpu.VMEM((128, 512), BF16), pltpu.VME...]
where the time goes in v3:
time: 66.7 us; the launch traced here: 66.6 us
  Pallas kernels  66 us (99%)
    pallas_call x1, Pallas kernels, local(): pl.pallas_call(kernel, out_shape=(pltpu.VMEM((128, 512), BF16), pltpu.VME...  64.6 us
    pallas_call x1, Pallas kernels, local(): pl.pallas_call(write_kernel, out_shape=(jax.ShapeDtypeStruct((128, 512),...  1.4 us

profile of v3, /device:TPU:1, one launch (start us, length us, event | category | flops | bytes accessed | tf_op | source)
XLA Modules:
  0.0 66.6 jit_solution(7884919516399518025)
XLA Ops:
  0.6 64.6 %sage_backward.1 = (bf16[128,512]{1,0:T(8,128)(2,1)S(1)}, bf16[2,512,512]{2,1,0:T(8,128)(2,1)S(1)}) custom-call(bf16[128,512]{1,0:T(8,128)(2,1)} %feat_hbm.1, bf16[512,512]{1,0:T(8,128)(2,1)} %ws_hbm.1, bf16[512,512]{1,0:T(8,128)(2,1)} %wn_hbm.1, bf16[128,512]{1,0:T(8,128)(2,1)} %cot_hbm.1, s32[16,128]{1,0:T(8,128)} %bitcast.5, s32[8,64]{1,0:T(8,128)} %bitcast.6, ...), custom_call_target="tpu_custom_call" | custom-call | tf_op jit(solution)/shard_map/sage_backward/pallas_call | solution.py:341
  65.2 1.4 %write_results.1 = (bf16[128,512]{1,0:T(8,128)(2,1)}, f32[512,512]{1,0:T(8,128)}, f32[512,512]{1,0:T(8,128)}) custom-call(bf16[128,512]{1,0:T(8,128)(2,1)S(1)} %get-tuple-element.5.gfeat_in, bf16[2,512,512]{2,1,0:T(8,128)(2,1)S(1)} %get-tuple-element.6.gw_in), custom_call_target="tpu_custom_call" | custom-call | tf_op jit(solution)/shard_map/write_results/pallas_call | solution.py:389

commit v4 on v3

--- a/solution.py
+++ b/solution.py
@@ -13,7 +13,7 @@
 
 
 STRIPS = ((0, 256, "xzy"), (256, 128, "zxy"), (384, 128, "yxz"))
-BATCHES = (((1, 16, 1),), ((16, 32, 1),), ((32, 48, 1),), ((48, 64, 1),))
+BATCHES = ((), ((1, 32, 1),), (), (), ((32, 64, 1),), ())
 
 
 def dot(left, right, left_dim=1, right_dim=0):
@@ -225,8 +225,10 @@
                 i = lax.rem(me2 + r, n2)
                 remote(two_out[s].at[part(i, 16)], two_in[s].at[part(me2, 16)], two_send.at[s],
                        two_recv.at[s], at2(i)).start()
-
-    send_boundary(back_ref, ret_ref, 1, *BATCHES[1])
+            if s == 0:
+                send_boundary(back_ref, ret_ref, 1, *BATCHES[1])
+
+    send_boundary(back_ref, ret_ref, 1, *BATCHES[2])
 
     for s, (_, _, _, (n2, me2, _), (n3, me3, at3)) in enumerate(strips):
         with jax.named_scope("step_three_%d" % s):
@@ -240,7 +242,7 @@
                 remote(here, here, three_send.at[s], three_recv.at[s],
                        at3(lax.rem(me3 + r, n3))).start()
 
-    send_boundary(back_ref, ret_ref, 1, *BATCHES[2])
+    send_boundary(back_ref, ret_ref, 1, *BATCHES[3])
 
     def final(s, rows, count):
         first, width = strips[s][:2]
@@ -258,7 +260,7 @@
                 remote(final(s, row, 16), final(s, row, 16), ag1_send.at[s], ag1_recv.at[s],
                        at2(lax.rem(me2 + r, n2))).start()
 
-    send_boundary(back_ref, ret_ref, 1, *BATCHES[3])
+    send_boundary(back_ref, ret_ref, 1, *BATCHES[4])
 
     def forward(s, unit, row, count):
         remote(final(s, row, count), final(s, row, count), fin_send.at[s, unit],
@@ -275,6 +277,8 @@
                        ag2_recv.at[s, unit], at1(lax.rem(me1 + r, n1))).start()
             if n1 == 4:
                 forward(s, me1, row, rows1)
+    send_boundary(back_ref, ret_ref, 1, *BATCHES[5])
+
     with jax.named_scope("forward"):
         for s, (_, _, (n1, me1, _), _, _) in enumerate(strips):
             if n1 == 4:

time: 66.7 us -> 65.9 us (0.988)
  Pallas kernels: 66 us -> 65.1 us
    pallas_call x1, Pallas kernels: 64.6 us -> 63.7 us  [local(): pl.pallas_call(kernel, out_shape=(pltpu.VMEM((128, 512), BF16), pltpu.VME...]
where the time goes in v4:
time: 65.9 us; the launch traced here: 65.8 us
  Pallas kernels  65.1 us (99%)
    pallas_call x1, Pallas kernels, local(): pl.pallas_call(kernel, out_shape=(pltpu.VMEM((128, 512), BF16), pltpu.VME...  63.7 us
    pallas_call x1, Pallas kernels, local(): pl.pallas_call(write_kernel, out_shape=(jax.ShapeDtypeStruct((128, 512),...  1.4 us

profile of v4, /device:TPU:1, one launch (start us, length us, event | category | flops | bytes accessed | tf_op | source)
XLA Modules:
  0.0 65.8 jit_solution(11401644328406400485)
XLA Ops:
  0.6 63.7 %sage_backward.1 = (bf16[128,512]{1,0:T(8,128)(2,1)S(1)}, bf16[2,512,512]{2,1,0:T(8,128)(2,1)S(1)}) custom-call(bf16[128,512]{1,0:T(8,128)(2,1)} %feat_hbm.1, bf16[512,512]{1,0:T(8,128)(2,1)} %ws_hbm.1, bf16[512,512]{1,0:T(8,128)(2,1)} %wn_hbm.1, bf16[128,512]{1,0:T(8,128)(2,1)} %cot_hbm.1, s32[16,128]{1,0:T(8,128)} %bitcast.5, s32[8,64]{1,0:T(8,128)} %bitcast.6, ...), custom_call_target="tpu_custom_call" | custom-call | tf_op jit(solution)/shard_map/sage_backward/pallas_call | solution.py:345
  64.4 1.4 %write_results.1 = (bf16[128,512]{1,0:T(8,128)(2,1)}, f32[512,512]{1,0:T(8,128)}, f32[512,512]{1,0:T(8,128)}) custom-call(bf16[128,512]{1,0:T(8,128)(2,1)S(1)} %get-tuple-element.5.gfeat_in, bf16[2,512,512]{2,1,0:T(8,128)(2,1)S(1)} %get-tuple-element.6.gw_in), custom_call_target="tpu_custom_call" | custom-call | tf_op jit(solution)/shard_map/write_results/pallas_call | solution.py:393

commit v5 on v4

--- a/solution.py
+++ b/solution.py
@@ -13,7 +13,7 @@
 
 
 STRIPS = ((0, 256, "xzy"), (256, 128, "zxy"), (384, 128, "yxz"))
-BATCHES = ((), ((1, 32, 1),), (), (), ((32, 64, 1),), ())
+BATCHES = ((), ((0, 31),), (), (), ((31, 63),), ())
 
 
 def dot(left, right, left_dim=1, right_dim=0):
@@ -36,11 +36,11 @@
 def kernel(
     feat_hbm, ws_hbm, wn_hbm, cot_hbm, nb_hbm, rows_hbm, count_hbm,
     gfeat_ref, gw_ref,
-    feat_ref, ws_ref, wn_ref, cot_ref, nb_ref, rows_ref, count_ref,
+    feat_ref, w_ref, cot_ref, nb_ref, rows_ref, count_ref,
     sel_ref, adj_ref, adjt_ref, out_ref, halo_ref, back_ref, ret_ref,
-    lt_ref, own_ref, pair_out, pair_in, one_out, one_in, sum_ref, two_out, two_in, three_ref, base_ref,
-    load_sem, a2a_send, a2a_recv, pair_send, pair_recv, one_send, one_recv, two_send, two_recv,
-    three_send, three_recv, ag1_send, ag1_recv, ag2_send, ag2_recv, fin_send, fin_recv,
+    lt_ref, lt_pair, gp_ref, own_ref, one_out, one_in, sum_ref, two_out, two_in, three_ref, base_ref,
+    all_sent_ref, load_sem, sent, a2a_recv, pair_recv, one_recv, two_recv, three_recv, ag1_recv,
+    ag2_recv, fin_recv,
 ):
     grp = lax.axis_index("grp")
     dom = lax.axis_index("dom")
@@ -61,12 +61,19 @@
     def dom_peer(r):
         return lax.rem(dom + r, 64)
 
+    def far_peer(q):
+        i = lax.rem(q, 8)
+        dy = 4 + (i + 1) // 2 * (1 - 2 * lax.rem(i, 2))
+        o = 7 - q // 8
+        return (
+            lax.rem(x + o // 2, 4) * 16 + lax.rem(y + dy, 8) * 2 + lax.rem(core + lax.rem(o, 2), 2))
+
     def loop(first, last, body):
         lax.fori_loop(first, last, lambda i, c: (body(i), c)[1], 0)
 
-    def remote(src, dst, send, recv, device):
+    def remote(src, dst, recv, device):
         return pltpu.make_async_remote_copy(
-            src_ref=src, dst_ref=dst, send_sem=send, recv_sem=recv,
+            src_ref=src, dst_ref=dst, send_sem=sent, recv_sem=recv,
             device_id=device, device_id_type=MESH,
         )
 
@@ -78,10 +85,11 @@
 
     loads = [
         pltpu.make_async_copy(src, dst, load_sem.at[i])
-        for i, (src, dst) in enumerate([
-            (rows_hbm, rows_ref), (count_hbm, count_ref), (feat_hbm, feat_ref), (nb_hbm, nb_ref),
-            (ws_hbm, ws_ref), (wn_hbm, wn_ref), (cot_hbm, cot_ref),
-        ])
+        for i, src, dst in [
+            (0, rows_hbm, rows_ref), (1, count_hbm, count_ref), (2, feat_hbm, feat_ref),
+            (3, nb_hbm, nb_ref), (4, cot_hbm, cot_ref),
+            (5, ws_hbm, w_ref.at[0]), (5, wn_hbm, w_ref.at[1]),
+        ]
     ]
     for load in loads:
         load.start()
@@ -117,11 +125,11 @@
 
     def send_boundary(src, dst, k, *distances):
         def one(r):
-            peer = dom_peer(r)
-            remote(src.at[part(peer, 16)], dst.at[part(dom, 16)], a2a_send.at[k], a2a_recv.at[k],
+            peer = far_peer(r) if k == 0 else dom_peer(r + 1)
+            remote(src.at[part(peer, 16)], dst.at[part(dom, 16)], a2a_recv.at[k],
                    {"dom": peer}).start()
-        for first, last, step in distances:
-            loop(0, (last - first) // step, lambda i: one(first + step * i))
+        for first, last in distances:
+            loop(first, last, one)
 
     def keep_boundary(src, dst):
         dst[part(dom, 16), :] = src[part(dom, 16), :]
@@ -130,7 +138,7 @@
         wait(dst.at[pl.ds(0, 63 * 16)], a2a_recv.at[k])
 
     with jax.named_scope("send_rows"):
-        send_boundary(out_ref, halo_ref, 0, (1, 64, 1))
+        send_boundary(out_ref, halo_ref, 0, (0, 63))
         keep_boundary(out_ref, halo_ref)
 
     with jax.named_scope("adjacency"):
@@ -156,9 +164,9 @@
         own_adj_t = own_t.astype(BF16)
         own_sum = dot(own_adj, feat)
         lt_ref[0] = feat.astype(F32).T.astype(BF16)
-        for load in loads[4:]:
-            load.wait()
-        pre_self = dot(feat, ws_ref[...])
+        loads[4].wait()
+        wait(w_ref, load_sem.at[5])
+        pre_self = dot(feat, w_ref[0])
 
     with jax.named_scope("wait_rows"):
         wait_boundary(halo_ref, 0)
@@ -166,56 +174,56 @@
         halo_sum = dot(adj_ref[...], halo_ref[...])
         summed = own_sum + jnp.concatenate([halo_sum[0:128], halo_sum[128:256]], axis=1)
         agg = (summed * (1.0 / 16.0)).astype(BF16)
-        pre = pre_self + dot(agg, wn_ref[...])
+        lt_ref[1] = agg.astype(F32).T.astype(BF16)
+        remote(lt_ref.at[other], lt_pair, pair_recv.at[0], sibling).start()
+        pre = pre_self + dot(agg, w_ref[1])
         grad_pre = (cot_ref[...].astype(F32) * gelu_slope(pre)).astype(BF16)
-
-    with jax.named_scope("weight_grads"):
-        lt_ref[1] = agg.astype(F32).T.astype(BF16)
-        scale = 65536.0 ** -0.5
-        pair_out[...] = (dot(lt_ref[other], grad_pre) * scale).astype(BF16)
-        for r in range(4):
-            i = lax.rem(x + 1 + r, 4)
-            remote(pair_out.at[part(i, 128)], pair_in.at[part(i, 128)], pair_send.at[i],
-                   pair_recv.at[i], sibling).start()
-        own_ref[...] = dot(lt_ref[core], grad_pre) * scale
+        gp_ref[0:128, :] = grad_pre
+        remote(gp_ref.at[pl.ds(0, 128)], gp_ref.at[pl.ds(128, 128)], pair_recv.at[1],
+               sibling).start()
 
     with jax.named_scope("boundary_grads"):
-        grad_agg = (dot(grad_pre, wn_ref[...], 1, 1) * (1.0 / 16.0)).astype(BF16)
+        grad_agg = (dot(grad_pre, w_ref[1], 1, 1) * (1.0 / 16.0)).astype(BF16)
         grad_agg2 = jnp.concatenate([grad_agg[:, :256], grad_agg[:, 256:]], axis=0)
         back_ref[...] = dot(adjt_ref[...], grad_agg2).astype(BF16)
 
     def send_one(s, i):
         first, width, (n, me, at), _, _ = strips[s]
         rows = part(i, 512 // n)
-        cols = pl.ds(first, width)
-        one_out[s][rows, :] = (
-            own_ref[rows, cols] + pair_in[rows, cols].astype(F32)).astype(BF16)
+        one_out[s][rows, :] = own_ref[rows, pl.ds(first, width)].astype(BF16)
 
         @pl.when(i != me)
         def _():
-            remote(one_out[s].at[rows], one_in[s].at[part(me, 512 // n)], one_send.at[s],
-                   one_recv.at[s], at(i)).start()
+            remote(one_out[s].at[rows], one_in[s].at[part(me, 512 // n)], one_recv.at[s],
+                   at(i)).start()
 
     with jax.named_scope("step_one"):
+        wait(lt_pair, pair_recv.at[0])
+        wait(gp_ref.at[pl.ds(0, 128)], pair_recv.at[1])
+        both = gp_ref[...]
+        scale = 65536.0 ** -0.5
         for r in range(4):
             i = lax.rem(x + 1 + r, 4)
-            wait(pair_in.at[part(i, 128)], pair_recv.at[i])
+            rows = part(i, 128)
+            left = jnp.concatenate([lt_ref[core, rows, :], lt_pair[rows, :]], axis=1)
+            own_ref[rows, :] = dot(left, both) * scale
             for s, (_, _, (n1, _, _), _, _) in enumerate(strips):
-                for j in range(n1 // 4):
-                    send_one(s, n1 // 4 * i + j)
+                if n1 == 8 or r < 3:
+                    for j in range(n1 // 4):
+                        send_one(s, n1 // 4 * i + j)
 
     with jax.named_scope("send_grads"):
         send_boundary(back_ref, ret_ref, 1, *BATCHES[0])
         keep_boundary(back_ref, ret_ref)
     with jax.named_scope("base"):
-        base_ref[...] = dot(grad_pre, ws_ref[...], 1, 1) + dot(own_adj_t, grad_agg)
+        base_ref[...] = dot(grad_pre, w_ref[0], 1, 1) + dot(own_adj_t, grad_agg)
 
     for s, (first, width, (n1, me1, _), (n2, me2, at2), _) in enumerate(strips):
         with jax.named_scope("step_two_%d" % s):
             rows1 = 512 // n1
             mine = part(me1, rows1)
             cols = pl.ds(first, width)
-            total = own_ref[mine, cols] + pair_in[mine, cols].astype(F32)
+            total = own_ref[mine, cols]
             wait(one_in[s].at[pl.ds(0, 512 - rows1)], one_recv.at[s])
             for r in range(1, n1):
                 total = total + one_in[s][part(lax.rem(me1 + r, n1), rows1), :].astype(F32)
@@ -223,7 +231,7 @@
             two_out[s][...] = total.astype(BF16)
             for r in range(1, n2):
                 i = lax.rem(me2 + r, n2)
-                remote(two_out[s].at[part(i, 16)], two_in[s].at[part(me2, 16)], two_send.at[s],
+                remote(two_out[s].at[part(i, 16)], two_in[s].at[part(me2, 16)],
                        two_recv.at[s], at2(i)).start()
             if s == 0:
                 send_boundary(back_ref, ret_ref, 1, *BATCHES[1])
@@ -239,7 +247,7 @@
             three_ref[s][part(me3, 16), :] = small.astype(BF16)
             for r in range(1, n3):
                 here = three_ref[s].at[part(me3, 16)]
-                remote(here, here, three_send.at[s], three_recv.at[s],
+                remote(here, here, three_recv.at[s],
                        at3(lax.rem(me3 + r, n3))).start()
 
     send_boundary(back_ref, ret_ref, 1, *BATCHES[3])
@@ -257,14 +265,17 @@
             row = pl.multiple_of(me1 * (512 // n1) + me2 * 16, 16)
             gw_ref[core, pl.ds(row, 16), pl.ds(first, width)] = done.astype(BF16)
             for r in range(1, n2):
-                remote(final(s, row, 16), final(s, row, 16), ag1_send.at[s], ag1_recv.at[s],
+                remote(final(s, row, 16), final(s, row, 16), ag1_recv.at[s],
                        at2(lax.rem(me2 + r, n2))).start()
 
     send_boundary(back_ref, ret_ref, 1, *BATCHES[4])
 
-    def forward(s, unit, row, count):
-        remote(final(s, row, count), final(s, row, count), fin_send.at[s, unit],
-               fin_recv.at[s, unit], sibling).start()
+    def forward(s, row, count):
+        remote(final(s, row, count), final(s, row, count), fin_recv, sibling).start()
+
+    units = []
+    for s, (_, _, (n1, _, _), _, _) in enumerate(strips):
+        units.append(units[-1] + (4 if strips[s - 1][2][0] == 4 else 1) if s else 0)
 
     for s, (_, _, (n1, me1, at1), (n2, _, _), _) in enumerate(strips):
         with jax.named_scope("gather_two_%d" % s):
@@ -272,11 +283,12 @@
             wait(final(s, 0, 16 * (n2 - 1)), ag1_recv.at[s])
             row = pl.multiple_of(me1 * rows1, rows1)
             for r in range(1, n1):
-                unit = me1 if n1 == 4 else 0
-                remote(final(s, row, rows1), final(s, row, rows1), ag2_send.at[s],
-                       ag2_recv.at[s, unit], at1(lax.rem(me1 + r, n1))).start()
+                unit = units[s] + me1 if n1 == 4 else units[s]
+                remote(final(s, row, rows1), final(s, row, rows1), ag2_recv.at[unit],
+                       at1(lax.rem(me1 + r, n1))).start()
             if n1 == 4:
-                forward(s, me1, row, rows1)
+                forward(s, row, rows1)
+
     send_boundary(back_ref, ret_ref, 1, *BATCHES[5])
 
     with jax.named_scope("forward"):
@@ -285,11 +297,11 @@
                 for r in range(1, 4):
                     i = lax.rem(me1 + r, 4)
                     row = pl.multiple_of(i * 128, 128)
-                    wait(final(s, row, 128), ag2_recv.at[s, i])
-                    forward(s, i, row, 128)
+                    wait(final(s, row, 128), ag2_recv.at[units[s] + i])
+                    forward(s, row, 128)
             else:
-                wait(final(s, 0, 448), ag2_recv.at[s, 0])
-                forward(s, 0, 0, 512)
+                wait(final(s, 0, 448), ag2_recv.at[units[s]])
+                forward(s, 0, 512)
 
     with jax.named_scope("wait_grads"):
         wait_boundary(ret_ref, 1)
@@ -300,21 +312,8 @@
         ).astype(BF16)
 
     with jax.named_scope("finish"):
-        wait(out_ref.at[pl.ds(0, 63 * 16)], a2a_send.at[0])
-        wait(back_ref.at[pl.ds(0, 63 * 16)], a2a_send.at[1])
-        for i in range(4):
-            wait(pair_out.at[pl.ds(128 * i, 128)], pair_send.at[i])
-        for s, (_, _, (n1, _, _), (n2, _, _), (n3, _, _)) in enumerate(strips):
-            rows1 = 512 // n1
-            wait(one_out[s].at[pl.ds(0, 512 - rows1)], one_send.at[s])
-            wait(two_out[s].at[pl.ds(0, 16 * (n2 - 1))], two_send.at[s])
-            wait(three_ref[s].at[pl.ds(0, 16 * (n3 - 1))], three_send.at[s])
-            wait(final(s, 0, 16 * (n2 - 1)), ag1_send.at[s])
-            wait(final(s, 0, 512 - rows1), ag2_send.at[s])
-            units = 4 if n1 == 4 else 1
-            for unit in range(units):
-                wait(final(s, 0, 512 // units), fin_send.at[s, unit])
-                wait(final(s, 0, 512 // units), fin_recv.at[s, unit])
+        wait(all_sent_ref, sent)
+        wait(gw_ref.at[other], fin_recv)
 
 
 def write_kernel(gfeat_in, gw_in, gfeat_ref, gws_ref, gwn_ref, wide_ref, sem):
@@ -336,6 +335,16 @@
     return tuple(
         pltpu.VMEM(shape(width, 4 if order[0] == "x" else 8), dtype) for _, width, order in STRIPS
     )
+
+
+def sent_rows():
+    length = {"x": 4, "y": 8, "z": 8}
+    rows = 2 * 63 * 8 + 2 * 128 + 512
+    for _, width, order in STRIPS:
+        n1, n2, n3 = (length[axis] for axis in order)
+        steps = 2 * (512 - 512 // n1) + 2 * 16 * (n2 - 1) + 16 * (n3 - 1)
+        rows += steps * width // 512
+    return rows
 
 
 def local(features, w_self, w_neigh, cotangent, neighbors, send_rows, send_count):
@@ -352,8 +361,7 @@
         out_specs=(vmem, vmem),
         scratch_shapes=[
             pltpu.VMEM((128, 512), BF16),
-            pltpu.VMEM((512, 512), BF16),
-            pltpu.VMEM((512, 512), BF16),
+            pltpu.VMEM((2, 512, 512), BF16),
             pltpu.VMEM((128, 512), BF16),
             pltpu.VMEM((16, 128), jnp.int32),
             pltpu.VMEM((8, 64), jnp.int32),
@@ -366,9 +374,9 @@
             pltpu.VMEM((1024, 256), BF16),
             pltpu.VMEM((1024, 256), BF16),
             pltpu.VMEM((2, 512, 128), BF16),
+            pltpu.VMEM((512, 128), BF16),
+            pltpu.VMEM((256, 512), BF16),
             pltpu.VMEM((512, 512), F32),
-            pltpu.VMEM((512, 512), BF16),
-            pltpu.VMEM((512, 512), BF16),
             strip_scratch(lambda w, n: (512, w), BF16),
             strip_scratch(lambda w, n: (512, w), BF16),
             strip_scratch(lambda w, n: (512 // n, w), F32),
@@ -376,8 +384,9 @@
             strip_scratch(lambda w, n: (512 // n, w), BF16),
             strip_scratch(lambda w, n: (128, w), BF16),
             pltpu.VMEM((128, 512), F32),
-            dma((7,)), dma((2,)), dma((2,)), dma((4,)), dma((4,)),
-            *([dma((len(STRIPS),))] * 9), *([dma((len(STRIPS), 4))] * 3),
+            pltpu.VMEM((sent_rows(), 512), BF16),
+            dma((6,)), dma, dma((2,)), dma((2,)), *([dma((len(STRIPS),))] * 4),
+            dma((sum(4 if order[0] == "x" else 1 for _, _, order in STRIPS),)), dma,
         ],
         compiler_params=pltpu.CompilerParams(
             collective_id=0, has_side_effects=True, vmem_limit_bytes=40 << 20

time: 65.9 us -> 64.2 us (0.974)
  Pallas kernels: 65.1 us -> 63.5 us
    pallas_call x1, Pallas kernels: 63.7 us -> 62.1 us  [local(): pl.pallas_call(kernel, out_shape=(pltpu.VMEM((128, 512), BF16), pltpu.VME...]
where the time goes in v5:
time: 64.2 us; the launch traced here: 64.1 us
  Pallas kernels  63.5 us (99%)
    pallas_call x1, Pallas kernels, local(): pl.pallas_call(kernel, out_shape=(pltpu.VMEM((128, 512), BF16), pltpu.VME...  62.1 us
    pallas_call x1, Pallas kernels, local(): pl.pallas_call(write_kernel, out_shape=(jax.ShapeDtypeStruct((128, 512),...  1.4 us

profile of v5, /device:TPU:1, one launch (start us, length us, event | category | flops | bytes accessed | tf_op | source)
XLA Modules:
  0.0 64.1 jit_solution(363388942300498895)
XLA Ops:
  0.6 62.1 %sage_backward.1 = (bf16[128,512]{1,0:T(8,128)(2,1)S(1)}, bf16[2,512,512]{2,1,0:T(8,128)(2,1)S(1)}) custom-call(bf16[128,512]{1,0:T(8,128)(2,1)} %feat_hbm.1, bf16[512,512]{1,0:T(8,128)(2,1)} %ws_hbm.1, bf16[512,512]{1,0:T(8,128)(2,1)} %wn_hbm.1, bf16[128,512]{1,0:T(8,128)(2,1)} %cot_hbm.1, s32[16,128]{1,0:T(8,128)} %bitcast.5, s32[8,64]{1,0:T(8,128)} %bitcast.6, ...), custom_call_target="tpu_custom_call" | custom-call | tf_op jit(solution)/shard_map/sage_backward/pallas_call | solution.py:354
  62.7 1.4 %write_results.1 = (bf16[128,512]{1,0:T(8,128)(2,1)}, f32[512,512]{1,0:T(8,128)}, f32[512,512]{1,0:T(8,128)}) custom-call(bf16[128,512]{1,0:T(8,128)(2,1)S(1)} %get-tuple-element.5.gfeat_in, bf16[2,512,512]{2,1,0:T(8,128)(2,1)S(1)} %get-tuple-element.6.gw_in), custom_call_target="tpu_custom_call" | custom-call | tf_op jit(solution)/shard_map/write_results/pallas_call | solution.py:402

commit v6 on v5

--- a/solution.py
+++ b/solution.py
@@ -13,7 +13,7 @@
 
 
 STRIPS = ((0, 256, "xzy"), (256, 128, "zxy"), (384, 128, "yxz"))
-BATCHES = ((), ((0, 31),), (), (), ((31, 63),), ())
+BATCHES = (((0, 15),), ((15, 31),), (), ((31, 47),), ((47, 63),), ())
 
 
 def dot(left, right, left_dim=1, right_dim=0):
@@ -238,7 +238,8 @@
 
     send_boundary(back_ref, ret_ref, 1, *BATCHES[2])
 
-    for s, (_, _, _, (n2, me2, _), (n3, me3, at3)) in enumerate(strips):
+    for s in sorted(range(len(strips)), key=lambda s: strips[s][2][0] == 4):
+        _, _, _, (n2, me2, _), (n3, me3, at3) = strips[s]
         with jax.named_scope("step_three_%d" % s):
             small = sum_ref[s][part(me2, 16), :]
             wait(two_in[s].at[pl.ds(0, 16 * (n2 - 1))], two_recv.at[s])
@@ -277,7 +278,8 @@
     for s, (_, _, (n1, _, _), _, _) in enumerate(strips):
         units.append(units[-1] + (4 if strips[s - 1][2][0] == 4 else 1) if s else 0)
 
-    for s, (_, _, (n1, me1, at1), (n2, _, _), _) in enumerate(strips):
+    for s in sorted(range(len(strips)), key=lambda s: strips[s][2][0] == 4):
+        _, _, (n1, me1, at1), (n2, _, _), _ = strips[s]
         with jax.named_scope("gather_two_%d" % s):
             rows1 = 512 // n1
             wait(final(s, 0, 16 * (n2 - 1)), ag1_recv.at[s])
@@ -320,11 +322,11 @@
     copies = [pltpu.make_async_copy(gfeat_in, gfeat_ref, sem.at[0])]
     copies[0].start()
     for c, ref in enumerate((gws_ref, gwn_ref)):
-        for half in range(2):
-            rows = pl.ds(256 * half, 256)
+        for piece in range(4):
+            rows = pl.ds(128 * piece, 128)
             wide_ref[c, rows, :] = gw_in[c, rows, :].astype(F32)
             copy = pltpu.make_async_copy(
-                wide_ref.at[c, rows], ref.at[rows], sem.at[1 + 2 * c + half])
+                wide_ref.at[c, rows], ref.at[rows], sem.at[1 + 4 * c + piece])
             copy.start()
             copies.append(copy)
     for copy in copies:
@@ -408,7 +410,7 @@
         ),
         in_specs=[vmem, vmem],
         out_specs=(hbm, hbm, hbm),
-        scratch_shapes=[pltpu.VMEM((2, 512, 512), F32), dma((5,))],
+        scratch_shapes=[pltpu.VMEM((2, 512, 512), F32), dma((9,))],
         compiler_params=pltpu.CompilerParams(vmem_limit_bytes=8 << 20),
         name="write_results",
     )(grad_features, grads)

time: 64.2 us -> 64.3 us (level)
  no operation moved by 1% of the time
where the time goes in v6:
time: 64.3 us; the launch traced here: 64.2 us
  Pallas kernels  63.6 us (99%)
    pallas_call x1, Pallas kernels, local(): pl.pallas_call(kernel, out_shape=(pltpu.VMEM((128, 512), BF16), pltpu.VME...  62.2 us
    pallas_call x1, Pallas kernels, local(): pl.pallas_call(write_kernel, out_shape=(jax.ShapeDtypeStruct((128, 512),...  1.43 us

profile of v6, /device:TPU:1, one launch (start us, length us, event | category | flops | bytes accessed | tf_op | source)
XLA Modules:
  0.0 64.2 jit_solution(5220353064181523725)
XLA Ops:
  0.6 62.2 %sage_backward.1 = (bf16[128,512]{1,0:T(8,128)(2,1)S(1)}, bf16[2,512,512]{2,1,0:T(8,128)(2,1)S(1)}) custom-call(bf16[128,512]{1,0:T(8,128)(2,1)} %feat_hbm.1, bf16[512,512]{1,0:T(8,128)(2,1)} %ws_hbm.1, bf16[512,512]{1,0:T(8,128)(2,1)} %wn_hbm.1, bf16[128,512]{1,0:T(8,128)(2,1)} %cot_hbm.1, s32[16,128]{1,0:T(8,128)} %bitcast.5, s32[8,64]{1,0:T(8,128)} %bitcast.6, ...), custom_call_target="tpu_custom_call" | custom-call | tf_op jit(solution)/shard_map/sage_backward/pallas_call | solution.py:356
  62.8 1.4 %write_results.1 = (bf16[128,512]{1,0:T(8,128)(2,1)}, f32[512,512]{1,0:T(8,128)}, f32[512,512]{1,0:T(8,128)}) custom-call(bf16[128,512]{1,0:T(8,128)(2,1)S(1)} %get-tuple-element.5.gfeat_in, bf16[2,512,512]{2,1,0:T(8,128)(2,1)S(1)} %get-tuple-element.6.gw_in), custom_call_target="tpu_custom_call" | custom-call | tf_op jit(solution)/shard_map/write_results/pallas_call | solution.py:404

commit v7 on v6

--- a/solution.py
+++ b/solution.py
@@ -13,7 +13,7 @@
 
 
 STRIPS = ((0, 256, "xzy"), (256, 128, "zxy"), (384, 128, "yxz"))
-BATCHES = (((0, 15),), ((15, 31),), (), ((31, 47),), ((47, 63),), ())
+BATCHES = ((), ((0, 31),), (), (), ((31, 63),), ())
 
 
 def dot(left, right, left_dim=1, right_dim=0):
@@ -61,10 +61,9 @@
     def dom_peer(r):
         return lax.rem(dom + r, 64)
 
-    def far_peer(q):
-        i = lax.rem(q, 8)
-        dy = 4 + (i + 1) // 2 * (1 - 2 * lax.rem(i, 2))
-        o = 7 - q // 8
+    far_first = (4, 3, 5, 2, 6, 1, 7, 0)
+
+    def far_peer(o, dy):
         return (
             lax.rem(x + o // 2, 4) * 16 + lax.rem(y + dy, 8) * 2 + lax.rem(core + lax.rem(o, 2), 2))
 
@@ -123,13 +122,20 @@
     with jax.named_scope("barrier"):
         pl.semaphore_wait(barrier, 70)
 
+    def send_block(src, dst, k, peer):
+        remote(src.at[part(peer, 16)], dst.at[part(dom, 16)], a2a_recv.at[k], {"dom": peer}).start()
+
+    def send_far_first(src, dst, k):
+        def one(i):
+            for dy in far_first:
+                send_block(src, dst, k, far_peer(7 - i, dy))
+        loop(0, 7, one)
+        for dy in far_first[:7]:
+            send_block(src, dst, k, far_peer(0, dy))
+
     def send_boundary(src, dst, k, *distances):
-        def one(r):
-            peer = far_peer(r) if k == 0 else dom_peer(r + 1)
-            remote(src.at[part(peer, 16)], dst.at[part(dom, 16)], a2a_recv.at[k],
-                   {"dom": peer}).start()
         for first, last in distances:
-            loop(first, last, one)
+            loop(first, last, lambda r: send_block(src, dst, k, dom_peer(r + 1)))
 
     def keep_boundary(src, dst):
         dst[part(dom, 16), :] = src[part(dom, 16), :]
@@ -138,7 +144,7 @@
         wait(dst.at[pl.ds(0, 63 * 16)], a2a_recv.at[k])
 
     with jax.named_scope("send_rows"):
-        send_boundary(out_ref, halo_ref, 0, (0, 63))
+        send_far_first(out_ref, halo_ref, 0)
         keep_boundary(out_ref, halo_ref)
 
     with jax.named_scope("adjacency"):
@@ -238,8 +244,7 @@
 
     send_boundary(back_ref, ret_ref, 1, *BATCHES[2])
 
-    for s in sorted(range(len(strips)), key=lambda s: strips[s][2][0] == 4):
-        _, _, _, (n2, me2, _), (n3, me3, at3) = strips[s]
+    for s, (_, _, _, (n2, me2, _), (n3, me3, at3)) in enumerate(strips):
         with jax.named_scope("step_three_%d" % s):
             small = sum_ref[s][part(me2, 16), :]
             wait(two_in[s].at[pl.ds(0, 16 * (n2 - 1))], two_recv.at[s])
@@ -278,8 +283,7 @@
     for s, (_, _, (n1, _, _), _, _) in enumerate(strips):
         units.append(units[-1] + (4 if strips[s - 1][2][0] == 4 else 1) if s else 0)
 
-    for s in sorted(range(len(strips)), key=lambda s: strips[s][2][0] == 4):
-        _, _, (n1, me1, at1), (n2, _, _), _ = strips[s]
+    for s, (_, _, (n1, me1, at1), (n2, _, _), _) in enumerate(strips):
         with jax.named_scope("gather_two_%d" % s):
             rows1 = 512 // n1
             wait(final(s, 0, 16 * (n2 - 1)), ag1_recv.at[s])

time: 64.3 us -> 64.3 us (level)
  no operation moved by 1% of the time
where the time goes in v7:
time: 64.3 us; the launch traced here: 64.1 us
  Pallas kernels  63.5 us (99%)
    pallas_call x1, Pallas kernels, local(): pl.pallas_call(kernel, out_shape=(pltpu.VMEM((128, 512), BF16), pltpu.VME...  62.1 us
    pallas_call x1, Pallas kernels, local(): pl.pallas_call(write_kernel, out_shape=(jax.ShapeDtypeStruct((128, 512),...  1.43 us

profile of v7, /device:TPU:1, one launch (start us, length us, event | category | flops | bytes accessed | tf_op | source)
XLA Modules:
  0.0 64.1 jit_solution(4275080590441307185)
XLA Ops:
  0.6 62.1 %sage_backward.1 = (bf16[128,512]{1,0:T(8,128)(2,1)S(1)}, bf16[2,512,512]{2,1,0:T(8,128)(2,1)S(1)}) custom-call(bf16[128,512]{1,0:T(8,128)(2,1)} %feat_hbm.1, bf16[512,512]{1,0:T(8,128)(2,1)} %ws_hbm.1, bf16[512,512]{1,0:T(8,128)(2,1)} %wn_hbm.1, bf16[128,512]{1,0:T(8,128)(2,1)} %cot_hbm.1, s32[16,128]{1,0:T(8,128)} %bitcast.5, s32[8,64]{1,0:T(8,128)} %bitcast.6, ...), custom_call_target="tpu_custom_call" | custom-call | tf_op jit(solution)/shard_map/sage_backward/pallas_call | solution.py:360
  62.7 1.4 %write_results.1 = (bf16[128,512]{1,0:T(8,128)(2,1)}, f32[512,512]{1,0:T(8,128)}, f32[512,512]{1,0:T(8,128)}) custom-call(bf16[128,512]{1,0:T(8,128)(2,1)S(1)} %get-tuple-element.5.gfeat_in, bf16[2,512,512]{2,1,0:T(8,128)(2,1)S(1)} %get-tuple-element.6.gw_in), custom_call_target="tpu_custom_call" | custom-call | tf_op jit(solution)/shard_map/write_results/pallas_call | solution.py:408

commit v8 on v7

--- a/solution.py
+++ b/solution.py
@@ -283,7 +283,8 @@
     for s, (_, _, (n1, _, _), _, _) in enumerate(strips):
         units.append(units[-1] + (4 if strips[s - 1][2][0] == 4 else 1) if s else 0)
 
-    for s, (_, _, (n1, me1, at1), (n2, _, _), _) in enumerate(strips):
+    for s in sorted(range(len(strips)), key=lambda s: strips[s][2][0] == 4):
+        _, _, (n1, me1, at1), (n2, _, _), _ = strips[s]
         with jax.named_scope("gather_two_%d" % s):
             rows1 = 512 // n1
             wait(final(s, 0, 16 * (n2 - 1)), ag1_recv.at[s])

time: 64.3 us -> 64.6 us (level)
  no operation moved by 1% of the time
where the time goes in v8:
time: 64.6 us; the launch traced here: 64.5 us
  Pallas kernels  63.8 us (99%)
    pallas_call x1, Pallas kernels, local(): pl.pallas_call(kernel, out_shape=(pltpu.VMEM((128, 512), BF16), pltpu.VME...  62.4 us
    pallas_call x1, Pallas kernels, local(): pl.pallas_call(write_kernel, out_shape=(jax.ShapeDtypeStruct((128, 512),...  1.43 us

profile of v8, /device:TPU:1, one launch (start us, length us, event | category | flops | bytes accessed | tf_op | source)
XLA Modules:
  0.0 64.5 jit_solution(12913002909637209804)
XLA Ops:
  0.6 62.4 %sage_backward.1 = (bf16[128,512]{1,0:T(8,128)(2,1)S(1)}, bf16[2,512,512]{2,1,0:T(8,128)(2,1)S(1)}) custom-call(bf16[128,512]{1,0:T(8,128)(2,1)} %feat_hbm.1, bf16[512,512]{1,0:T(8,128)(2,1)} %ws_hbm.1, bf16[512,512]{1,0:T(8,128)(2,1)} %wn_hbm.1, bf16[128,512]{1,0:T(8,128)(2,1)} %cot_hbm.1, s32[16,128]{1,0:T(8,128)} %bitcast.5, s32[8,64]{1,0:T(8,128)} %bitcast.6, ...), custom_call_target="tpu_custom_call" | custom-call | tf_op jit(solution)/shard_map/sage_backward/pallas_call | solution.py:361
  63.0 1.4 %write_results.1 = (bf16[128,512]{1,0:T(8,128)(2,1)}, f32[512,512]{1,0:T(8,128)}, f32[512,512]{1,0:T(8,128)}) custom-call(bf16[128,512]{1,0:T(8,128)(2,1)S(1)} %get-tuple-element.5.gfeat_in, bf16[2,512,512]{2,1,0:T(8,128)(2,1)S(1)} %get-tuple-element.6.gw_in), custom_call_target="tpu_custom_call" | custom-call | tf_op jit(solution)/shard_map/write_results/pallas_call | solution.py:409
